TPU v7x, 256 devices: a whole 4x4x8 slice. The times are simulated.
256 devices in a mesh: leaf: 64 (over y, z, core), tensor: 4 (over x).
Axes of the slice: x: 4, y: 4, z: 8, core: 2. Of those that a mesh axis runs over, the one named last changes fastest.
Arguments:
- queries: bfloat16 [2048, 32, 2048], P('leaf', None, 'tensor'), may hold values from -6 to 6
- keys: bfloat16 [2048, 32, 512], P('leaf', None, 'tensor'), may hold values from -6 to 6
- values: bfloat16 [2048, 32, 512], P('leaf', None, 'tensor'), may hold values from -6 to 6
- resid: bfloat16 [2048, 32, 4096], P('leaf', None, 'tensor'), may hold values from -6 to 6
- out_weight: bfloat16 [2048, 4096], P('tensor'), may hold values from -0.125 to 0.125
- norm_gain: bfloat16 [4096], P('tensor'), may hold values from 0.5 to 1.5
- value_weight: bfloat16 [4096], P('tensor'), may hold values from -0.09375 to 0.09375
- parent: int32 [2048], P('leaf'), may hold values from -1 to 2047, as said below
- counts: int32 [64], P('leaf'), may hold values from 25 to 32, as said below
Outputs:
- layer_out: bfloat16 [2048, 32, 4096], P('leaf', None, 'tensor')
- backed: float32 [2048], P('leaf')
Inputs may be any that keep to these rules, and one draw needn't show every extreme that they name: parent[n] is -1 for nodes of level 0 and for nodes that are not live; otherwise it is a live node of level one less. The parents of one device's nodes that lie on other devices lie on distinct devices. `counts`: every device holds at least 3 full levels.
All inputs are finite; a program needn't handle non-finite values.
Results may differ from a plain program's by a relative error of at most 0.008.
Values may be sent and summed in bfloat16 or wider, within the bound.
A program may use at most 128 MiB of HBM per device.

v0:
```python
import math

import jax
import jax.numpy as jnp
from jax import lax
from jax.sharding import PartitionSpec as P

D = 4096
DH = 128
BLK = 32
LEVELS = 4
W = 8


norm_eps = 1e-05
masked_score = -1e30


def pick_rows(source_rows, row_ids):
    clipped = jnp.clip(row_ids, 0, source_rows.shape[0] - 1)
    taken = jnp.take(source_rows, clipped, axis=0)
    return jnp.where((row_ids >= 0)[:, None, None], taken, jnp.zeros_like(taken))


def relay_round(source_rows, incoming, wanted_peer, local_slot):
    outgoing = pick_rows(source_rows, incoming)
    received = lax.all_to_all(outgoing, "leaf", split_axis=0, concat_axis=0, tiled=True)
    return pick_rows(received, wanted_peer) + pick_rows(source_rows, local_slot)


def body(queries, keys, values, resid, out_weight, norm_gain, value_weight, parent, counts):
    slot_count = parent.shape[0]
    leaf_count = lax.axis_size("leaf")
    leaf_index = lax.axis_index("leaf")
    block_len = queries.shape[1]
    head_cols = queries.shape[2]
    kv_cols = keys.shape[2]
    kv_here = kv_cols // DH
    group = head_cols // kv_cols
    width_cols = resid.shape[2]
    slot_ids = jnp.arange(slot_count, dtype=jnp.int32)
    node_level = slot_ids // W
    alive_slot = slot_ids < counts[0]
    global_ids = leaf_index * slot_count + slot_ids
    owner_dev = jnp.where(parent >= 0, parent // slot_count, -1)
    remote = (parent >= 0) & (owner_dev != leaf_index)
    local = (parent >= 0) & (owner_dev == leaf_index)
    wanted_peer = jnp.where(remote, owner_dev, -1)
    local_slot = jnp.where(local, parent % slot_count, -1)
    peer_ids = jnp.arange(leaf_count, dtype=jnp.int32)
    matching = remote[None, :] & (owner_dev[None, :] == peer_ids[:, None])
    asked = jnp.max(jnp.where(matching, (parent % slot_count)[None, :], -1), axis=1)
    incoming = lax.all_to_all(
        asked.reshape(leaf_count, 1), "leaf", split_axis=0, concat_axis=0, tiled=True
    ).reshape(leaf_count)
    own_rows = jnp.concatenate((keys, values), axis=2)
    source_rows = own_rows
    fetched = []
    for hop in range(LEVELS - 1):
        source_rows = relay_round(source_rows, incoming, wanted_peer, local_slot)
        fetched.append(source_rows)
    context = jnp.concatenate(fetched[::-1] + [own_rows], axis=1)
    key_slot = jnp.arange(LEVELS * block_len, dtype=jnp.int32)
    distance = LEVELS - 1 - key_slot // block_len
    query_slot = jnp.arange(block_len, dtype=jnp.int32)
    causal = (distance[None, :] == 0) & (key_slot[None, :] % block_len <= query_slot[:, None])
    ancestor_ok = (distance[None, :] >= 1) & (distance[None, :] <= node_level[:, None])
    allowed = ancestor_ok[:, None, None, None, :] | causal[None, None, None, :, :]
    query_heads = queries.reshape(slot_count, block_len, kv_here, group, DH)
    key_heads = context[:, :, :kv_cols].reshape(slot_count, LEVELS * block_len, kv_here, DH)
    value_heads = context[:, :, kv_cols:].reshape(slot_count, LEVELS * block_len, kv_here, DH)
    scores = jnp.einsum(
        "nqgrd,nkgd->ngrqk", query_heads, key_heads, preferred_element_type=jnp.float32
    ) * DH ** (-0.5)
    scores = jnp.where(allowed, scores, masked_score)
    highest = jnp.max(scores, axis=-1, keepdims=True)
    expo = jnp.exp(scores - highest)
    weights = (expo / jnp.sum(expo, axis=-1, keepdims=True)).astype(jnp.bfloat16)
    attended = jnp.einsum(
        "ngrqk,nkgd->nqgrd", weights, value_heads, preferred_element_type=jnp.float32
    )
    attended = attended.astype(jnp.bfloat16).reshape(slot_count * block_len, head_cols)
    partial_value = jnp.dot(attended, out_weight, preferred_element_type=jnp.float32)
    projected = lax.psum_scatter(partial_value, "tensor", scatter_dimension=1, tiled=True)
    resid_rows = resid.reshape(slot_count * block_len, width_cols)
    hidden = (resid_rows.astype(jnp.float32) + projected).astype(jnp.bfloat16)
    hidden_f = hidden.astype(jnp.float32)
    mixer = norm_gain.astype(jnp.float32) * value_weight.astype(jnp.float32)
    squares = jnp.sum(hidden_f * hidden_f, axis=-1)
    mixed = jnp.sum(hidden_f * mixer, axis=-1)
    squares, mixed = lax.psum((squares, mixed), "tensor")
    token_score = mixed / jnp.sqrt(squares / D + norm_eps)
    reward = jnp.tanh(jnp.sum(token_score.reshape(slot_count, block_len), axis=1) / math.sqrt(BLK))
    reward = jnp.where(alive_slot, reward, 0.0)
    layer_out = jnp.where(
        alive_slot[:, None, None],
        hidden.reshape(slot_count, block_len, width_cols),
        jnp.zeros((slot_count, block_len, width_cols), jnp.bfloat16),
    )
    parent_all = lax.all_gather(parent, "leaf", axis=0, tiled=True)
    is_child = (parent_all[None, :] == global_ids[:, None]).astype(jnp.float32)
    child_count = jnp.sum(is_child, axis=1)
    backed = reward
    for hop in range(LEVELS - 1):
        target_level = LEVELS - 2 - hop
        everyone = lax.all_gather(backed, "leaf", axis=0, tiled=True)
        child_sum = jnp.dot(is_child, everyone, precision=lax.Precision.HIGHEST)
        updated = jnp.where(
            child_count > 0, 0.5 * reward + 0.5 * child_sum / jnp.maximum(child_count, 1.0), reward
        )
        backed = jnp.where(node_level == target_level, updated, backed)
    backed = jnp.where(alive_slot, backed, 0.0)
    return (layer_out, backed)


def solution(mesh):
    in_specs = (
        P("leaf", None, "tensor"),
        P("leaf", None, "tensor"),
        P("leaf", None, "tensor"),
        P("leaf", None, "tensor"),
        P("tensor", None),
        P("tensor"),
        P("tensor"),
        P("leaf"),
        P("leaf"),
    )
    out_specs = (P("leaf", None, "tensor"), P("leaf"))
    return jax.shard_map(body, mesh=mesh, in_specs=in_specs, out_specs=out_specs, check_vma=False)
```

profile of v0, /device:TPU:1, one launch (start us, length us, event | category | flops | bytes accessed | tf_op | source)
XLA Modules:
  0.0 719.2 jit_solution(152858080899277383)
XLA Ops:
  9.4 13.2 %all-to-all-start = ((s32[64,1,1]{2,1,0:T(1,128)}), s32[64,1,1]{2,1,0:T(1,128)S(1)}, u32[]{:S(2)}, u32[]{:S(2)}) async-start(s32[64,1,1]{2,1,0:T(1,128)} %copy.20), calls=%async_computation | async-start | bytes 65536 | tf_op jit(solution)/shard_map/all_to_all | solution.py:53
  24.6 7.2 all-to-all-done
  36.1 4.8 all-to-all-start.1
  41.5 28.0 %all-to-all-done.1 = bf16[64,32,256]{2,1,0:T(8,128)(2,1)S(1)} async-done(((bf16[64,32,256]{2,1,0:T(8,128)(2,1)}), bf16[64,32,256]{2,1,0:T(8,128)(2,1)S(1)}, u32[]{:S(2)}, u32[]{:S(2)}) %all-to-all-start.1) | async-done | bytes 1048608 | tf_op jit(solution)/shard_map/all_to_all | solution.py:27
  69.5 1.4 gather_fusion.1
  73.9 6.3 all-to-all-start.2
  81.6 27.2 %all-to-all-done.2 = bf16[64,32,256]{2,1,0:T(8,128)(2,1)S(1)} async-done(((bf16[64,32,256]{2,1,0:T(8,128)(2,1)}), bf16[64,32,256]{2,1,0:T(8,128)(2,1)S(1)}, u32[]{:S(2)}, u32[]{:S(2)}) %all-to-all-start.2) | async-done | bytes 1048608 | tf_op jit(solution)/shard_map/all_to_all | solution.py:27
  108.8 1.4 gather_fusion.4
  110.1 1.4 fusion.29
  111.5 1.6 gather_fusion.6
  113.1 2.4 select_select_fusion
  115.5 6.4 all-to-all-start.3
  123.0 27.4 %all-to-all-done.3 = bf16[64,32,256]{2,1,0:T(8,128)(2,1)} async-done(((bf16[64,32,256]{2,1,0:T(8,128)(2,1)}), bf16[64,32,256]{2,1,0:T(8,128)(2,1)}, u32[]{:S(2)}, u32[]{:S(2)}) %all-to-all-start.3) | async-done | bytes 1048608 | tf_op jit(solution)/shard_map/all_to_all | solution.py:27
  150.4 2.6 gather_fusion.7
  156.8 1.9 fusion.4
  159.2 8.1 %fusion.21 = f32[1024,4096]{1,0:T(8,128)} fusion(bf16[512,4096]{1,0:T(8,128)(2,1)S(1)} %copy-done.4, bf16[128,8,4,128]{3,2,1,0:T(4,128)(2,1)S(1)} %bitcast.97), kind=kOutput, calls=%fused_computation.42 | convolution fusion | flops 4294967296 | bytes 22020096 | tf_op jit(solution)/shard_map/dot_general | solution.py:83
  169.6 14.1 %all-reduce = s32[2048]{0:T(1024)S(1)} all-reduce(s32[2048]{0:T(1024)S(1)} %dynamic-update-slice), channel_id=1, replica_groups=mesh['leaf'=64,'tensor'=4] {'leaf'}, use_global_device_ids=true, to_apply=%add | all-reduce | flops 2048 | bytes 16384
  183.9 130.9 %reduce-scatter.2.cloned.1.call-done = f32[1024,1024]{1,0:T(8,128)} async-done(((f32[1024,4096]{1,0:T(8,128)}), f32[1024,1024]{1,0:T(8,128)}) %reduce-scatter.2.cloned.1.call-update) | async-done | bytes 4194320 | tf_op jit(solution)/shard_map/reduce_scatter | solution.py:84
  314.8 3.9 fusion.1
  318.7 6.7 all-reduce.4
  325.7 128.6 %all-reduce.1 = f32[2048]{0:T(1024)S(1)} all-reduce(f32[2048]{0:T(1024)S(1)} %fusion.45), channel_id=1, replica_groups=mesh['leaf'=64,'tensor'=4] {'leaf'}, use_global_device_ids=true, to_apply=%add.1 | all-reduce | flops 2048 | bytes 16384
  454.9 128.5 %all-reduce.2 = f32[2048]{0:T(1024)S(1)} all-reduce(f32[2048]{0:T(1024)S(1)} %dynamic-update-slice.2), channel_id=1, replica_groups=mesh['leaf'=64,'tensor'=4] {'leaf'}, use_global_device_ids=true, to_apply=%add.2 | all-reduce | flops 2048 | bytes 16384
  583.9 126.1 %all-reduce.3 = f32[2048]{0:T(1024)S(1)} all-reduce(f32[2048]{0:T(1024)S(1)} %dynamic-update-slice.3), channel_id=1, replica_groups=mesh['leaf'=64,'tensor'=4] {'leaf'}, use_global_device_ids=true, to_apply=%add.3 | all-reduce | flops 2048 | bytes 16384
  710.8 1.5 broadcast_select_fusion
  (66 shorter events, 22.2 us)
Async XLA Ops:
  7.2 147.3 %copy-start = (bf16[32,32,512]{2,1,0:T(8,128)(2,1)S(1)}, bf16[32,32,512]{2,1,0:T(8,128)(2,1)}, u32[]{:S(2)}) copy-start(bf16[32,32,512]{2,1,0:T(8,128)(2,1)} %param.15) | copy-start | bytes 3145732
  9.4 22.4 %all-to-all-start = ((s32[64,1,1]{2,1,0:T(1,128)}), s32[64,1,1]{2,1,0:T(1,128)S(1)}, u32[]{:S(2)}, u32[]{:S(2)}) async-start(s32[64,1,1]{2,1,0:T(1,128)} %copy.20), calls=%async_computation | async-start | bytes 65536 | tf_op jit(solution)/shard_map/all_to_all | solution.py:53
  36.1 33.3 %all-to-all-start.1 = ((bf16[64,32,256]{2,1,0:T(8,128)(2,1)}), bf16[64,32,256]{2,1,0:T(8,128)(2,1)S(1)}, u32[]{:S(2)}, u32[]{:S(2)}) async-start(bf16[64,32,256]{2,1,0:T(8,128)(2,1)} %select_select_fusion.2), calls=%async_computation.1 | async-start | bytes 2097152 | tf_op jit(solution)/shard_map/all_to_all | solution.py:27
  73.9 34.9 %all-to-all-start.2 = ((bf16[64,32,256]{2,1,0:T(8,128)(2,1)}), bf16[64,32,256]{2,1,0:T(8,128)(2,1)S(1)}, u32[]{:S(2)}, u32[]{:S(2)}) async-start(bf16[64,32,256]{2,1,0:T(8,128)(2,1)} %select_select_fusion.1), calls=%async_computation.2 | async-start | bytes 2097152 | tf_op jit(solution)/shard_map/all_to_all | solution.py:27
  115.5 34.9 %all-to-all-start.3 = ((bf16[64,32,256]{2,1,0:T(8,128)(2,1)}), bf16[64,32,256]{2,1,0:T(8,128)(2,1)}, u32[]{:S(2)}, u32[]{:S(2)}) async-start(bf16[64,32,256]{2,1,0:T(8,128)(2,1)} %select_select_fusion), calls=%async_computation.3 | async-start | bytes 2097152 | tf_op jit(solution)/shard_map/all_to_all | solution.py:27
  121.9 192.9 %reduce-scatter.2.cloned.1.call-start = ((), (), s32[]{:S(2)}) async-start(), calls=%async_computation.5 | async-start | bytes 20971520 | tf_op jit(solution)/shard_map/reduce_scatter | solution.py:84
  156.8 2.4 copy-start.4
  167.3 0.7 copy-start.5
  167.3 2.0 copy-start.1
  167.3 16.6 %copy-start.2 = (bf16[1024]{0:T(1024)(128)(2,1)S(1)}, bf16[1024]{0:T(1024)(128)(2,1)}, u32[]{:S(2)}) copy-start(bf16[1024]{0:T(1024)(128)(2,1)} %param.21) | copy-start | bytes 6148
  167.3 16.6 %copy-start.3 = (bf16[1024]{0:T(1024)(128)(2,1)S(1)}, bf16[1024]{0:T(1024)(128)(2,1)}, u32[]{:S(2)}) copy-start(bf16[1024]{0:T(1024)(128)(2,1)} %param.20) | copy-start | bytes 6148
Sparse Core Ops, SparseCore 0:
  167.5 147.3 reduce-scatter.1
where the time goes:
time: 720 us; the launch traced here: 719 us
  blocking collectives  404 us (56%)
  waiting for transfers between devices  221 us (31%)
  starting transfers between devices  30.8 us (4%)
  other arithmetic  20.3 us (3%)
  between operations  15.7 us (2%)
  local copies, waits for them, and re-layouts  15.6 us (2%)
  matrix products  12.2 us (2%)
    unnamed x4, blocking collectives  397 us
    reduce_scatter x1, waiting for transfers between devices, body(): lax.psum_scatter(partial_value, 'tensor', scatter_dimension=1, tiled=True)  131 us
    all_to_all x3, waiting for transfers between devices, relay_round(): lax.all_to_all(outgoing, 'leaf', split_axis=0, concat_axis=0, tiled=True)  82.6 us
    all_to_all x3, starting transfers between devices, relay_round(): lax.all_to_all(outgoing, 'leaf', split_axis=0, concat_axis=0, tiled=True)  17.4 us
  transfers between devices with their start and end apart: 5, of which 5 were waited for; matrix products, arithmetic and copies ran while one was open for 1% of the time, Pallas kernels for 0%

commit v1 on v0

v1 whole, which is shorter than its diff:
```python
import math

import jax
import jax.numpy as jnp
from jax import lax
from jax.experimental import pallas as pl
from jax.experimental.pallas import tpu as pltpu
from jax.sharding import PartitionSpec as P

D = 4096
DH = 128
BLK = 32
LEVELS = 4
W = 8
NX, NY, NZ, NC = 4, 4, 8, 2
ZC = NZ * NC
SLOTS = LEVELS * W
HEADS_HERE = 4
ROWS = W * BLK
COLS = HEADS_HERE * DH
WIDTH = D // NX
WROWS = COLS // (NY * NC)
TILE = 256
HALF = W // 2
BATCHES = ((0, 1), (0, 2), (1, 2), (0, 3), (1, 3), (2, 3))

norm_eps = 1e-05
masked_score = -1e30
BF16 = jnp.bfloat16
F32 = jnp.float32
MESH = pl.DeviceIdType.MESH


def kernel(
    q_hbm, k_hbm, v_hbm, r_hbm, w_hbm, gain_ref, vw_ref, ptile_ref, counts_ref,
    hid_hbm, bk_ref,
    q_v, k_v, v_v, r_v, wf, kvg0, kvg1, kvg2, ag, ysa, ysp, ysm, yh, yr, hid_v,
    gp, ap, gr, ar, psm, pvm, amat, bmat, invm, keepm, stats, srecv, rtile, sqacc, mxacc,
    lsem, zs, zr, sbs, sbr, yas, yar, yfs, yfr, xs, xr, wxs, wxr, wys, wyr, wbs, wbr,
    g1s, g1r, g2s, g2r, sts, strv,
):
    kvg = (kvg0, kvg1, kvg2)
    leaf = lax.axis_index("leaf")
    x = lax.axis_index("tensor")
    c = lax.rem(leaf, NC)
    z = lax.rem(leaf // NC, NZ)
    y = leaf // ZC
    zc = lax.rem(leaf, ZC)

    def leaf_of(yy, zz, cc):
        return (yy * NZ + zz) * NC + cc

    def shift(v, d, n):
        return lax.rem(v + d + n, n)

    yp, ym, ya2 = shift(y, 1, NY), shift(y, -1, NY), shift(y, 2, NY)
    xp, xm, xa = shift(x, 1, NX), shift(x, -1, NX), shift(x, 2, NX)
    zp, zm = shift(z, 1, NZ), shift(z, -1, NZ)
    at_zp, at_zm = (leaf_of(y, zp, c), x), (leaf_of(y, zm, c), x)
    at_sib = (leaf_of(y, z, 1 - c), x)
    at_yp, at_ym, at_ya = (leaf_of(yp, z, c), x), (leaf_of(ym, z, c), x), (leaf_of(ya2, z, c), x)
    at_xp, at_xm, at_xa = (leaf, xp), (leaf, xm), (leaf, xa)

    def plane_peer(i):
        return (y * ZC + lax.rem(zc + i, ZC), x)

    started = []

    def remote(src, dst, ssem, rsem, dev):
        copy = pltpu.make_async_remote_copy(
            src_ref=src, dst_ref=dst, send_sem=ssem, recv_sem=rsem, device_id=dev, device_id_type=MESH
        )
        return copy

    def send(src, dst, ssem, rsem, dev):
        copy = remote(src, dst, ssem, rsem, dev)
        copy.start()
        started.append(copy)

    def arrived(ref, ssem, rsem):
        remote(ref, ref, ssem, rsem, at_sib).wait_recv()

    barrier = pltpu.get_barrier_semaphore()
    partners = [plane_peer(i) for i in range(1, ZC)] + [at_yp, at_ym, at_ya, at_xp, at_xm, at_xa]
    for dev in partners:
        pl.semaphore_signal(barrier, inc=1, device_id=dev, device_id_type=MESH)

    locals_ = []

    def local(src, dst):
        copy = pltpu.make_async_copy(src, dst, lsem.at[len(locals_)])
        copy.start()
        locals_.append(copy)
        return copy

    own_kv = []
    for l in range(3):
        own_kv.append(
            (
                local(k_hbm.at[pl.ds(W * l, W)], kvg[l].at[zc, 0]),
                local(v_hbm.at[pl.ds(W * l, W)], kvg[l].at[zc, 1]),
            )
        )
    in_q = local(q_hbm, q_v)
    in_k = local(k_hbm, k_v)
    in_v = local(v_hbm, v_v)
    in_w = local(w_hbm.at[:, pl.ds(pl.multiple_of(x * WIDTH, WIDTH), WIDTH)], wf.at[3])
    in_r = local(r_hbm, r_v)
    pl.semaphore_wait(barrier, len(partners))

    def gather_send(tile, buf, which):
        for i in range(1, ZC):
            send(tile, buf.at[zc], g1s.at[which, i], g1r.at[which, i], plane_peer(i))

    def gather_pass(tile, buf, whole, which):
        buf[zc] = tile[...]
        for i in range(1, ZC):
            arrived(buf.at[lax.rem(zc + ZC - i, ZC)], g1s.at[which, i], g1r.at[which, i])
        for half in range(2):
            total = buf[8 * half]
            for i in range(1, 8):
                total = total + buf[8 * half + i]
            whole[y, half] = total
        send(whole.at[y], whole.at[y], g2s.at[which, 0], g2r.at[which, 0], at_yp)
        send(whole.at[y], whole.at[y], g2s.at[which, 1], g2r.at[which, 1], at_ym)
        send(whole.at[y], whole.at[y], g2s.at[which, 2], g2r.at[which, 2], at_ya)

    def gather_end(whole, which):
        arrived(whole.at[ym], g2s.at[which, 0], g2r.at[which, 0])
        arrived(whole.at[yp], g2s.at[which, 1], g2r.at[which, 1])
        arrived(whole.at[ya2], g2s.at[which, 2], g2r.at[which, 2])

    def zidx(d, cc):
        return shift(z, d, NZ) * NC + cc

    def z_start(l):
        for copy in own_kv[l]:
            copy.wait()
        own = kvg[l].at[zc]
        send(own, own, zs.at[l, 0, 0], zr.at[l, 0, 0], at_zp)
        send(own, own, zs.at[l, 1, 0], zr.at[l, 1, 0], at_zm)
        send(own, own, sbs.at[l, 0], sbr.at[l, 0], at_sib)

    def z_step(l, s):
        for way, d in ((0, -s), (1, s)):
            shard = kvg[l].at[zidx(d, c)]
            part = shard if s < 4 else shard.at[way]
            arrived(part, zs.at[l, way, s - 1], zr.at[l, way, s - 1])
            if s < 4:
                onward = shard if s < 3 else shard.at[way]
                send(onward, onward, zs.at[l, way, s], zr.at[l, way, s], at_zm if way else at_zp)
                send(shard, shard, sbs.at[l, 1 + way * 3 + s - 1], sbr.at[l, 1 + way * 3 + s - 1], at_sib)
        if s == 4:
            shard = kvg[l].at[zidx(4, c)]
            send(shard, shard, sbs.at[l, 7], sbr.at[l, 7], at_sib)

    def z_end(l):
        for j, d in enumerate((0, -1, -2, -3, 1, 2, 3, 4)):
            arrived(kvg[l].at[zidx(d, 1 - c)], sbs.at[l, j], sbr.at[l, j])

    def climb(node, hops):
        for _ in range(hops):
            node = jnp.maximum(psm[lax.shift_right_logical(node, 5), node & 31], 0)
        return node

    def locate(dev, l, n, s):
        node = climb(dev * SLOTS + W * l + n, l - s)
        owner = lax.shift_right_logical(node, 5)
        return lax.shift_right_logical(owner, 4), owner & 15, node & 7

    def y_far(b):
        s, l = BATCHES[b]
        dev = ya2 * ZC + zc

        def pick(n, carry):
            _, src, slot = locate(dev, l, n, s)
            for kv in range(2):
                ysa[b, n, kv] = kvg[s][src, kv, slot]
            return carry

        lax.fori_loop(0, W, pick, 0)
        first, second = ysa.at[b, pl.ds(0, HALF)], ysa.at[b, pl.ds(HALF, HALF)]
        send(first, yh.at[b, 0], yas.at[b, 0], yar.at[b, 0], at_yp)
        send(second, yh.at[b, 1], yas.at[b, 1], yar.at[b, 1], at_ym)

    def y_near(b):
        s, l = BATCHES[b]
        arrived(yh.at[b, 0], yas.at[b, 0], yar.at[b, 0])
        arrived(yh.at[b, 1], yas.at[b, 1], yar.at[b, 1])
        dev_p = yp * ZC + zc
        dev_m = ym * ZC + zc

        def pick(n, carry):
            for half in range(2):
                row = half * HALF + n
                for out, dev, way in ((ysp, dev_p, 0), (ysm, dev_m, 1)):
                    col, src, slot = locate(dev, l, row, s)
                    for kv in range(2):
                        mine = kvg[s][src, kv, slot]
                        if half == way:
                            mine = jnp.where(col == y, mine, yh[b, way, n, kv])
                        out[b, row, kv] = mine
            return carry

        lax.fori_loop(0, HALF, pick, 0)
        send(ysp.at[b], yr.at[b, 0], yfs.at[b, 0], yfr.at[b, 0], at_yp)
        send(ysm.at[b], yr.at[b, 1], yfs.at[b, 1], yfr.at[b, 1], at_ym)

    def y_end(b):
        arrived(yr.at[b, 0], yfs.at[b, 0], yfr.at[b, 0])
        arrived(yr.at[b, 1], yfs.at[b, 1], yfr.at[b, 1])

    row_q = lax.broadcasted_iota(jnp.int32, (HEADS_HERE * BLK, LEVELS * BLK), 0) & (BLK - 1)
    key_j = lax.broadcasted_iota(jnp.int32, (HEADS_HERE * BLK, LEVELS * BLK), 1)

    def attention(l):
        allowed = ((key_j < BLK) & (key_j <= row_q)) | ((key_j >= BLK) & (key_j < BLK * (l + 1)))
        mine_dev = leaf

        def one(n, half):
            node = W * l + n
            q_node = q_v[node]
            q_rows = jnp.concatenate([q_node[:, h * DH : (h + 1) * DH] for h in range(HEADS_HERE)], axis=0)
            parts = [[k_v[node]], [v_v[node]]]
            for k in range(1, l + 1):
                s = l - k
                b = BATCHES.index((s, l))
                col, src, slot = locate(mine_dev, l, n, s)
                here = col == y
                if half == 0:
                    from_p = col == yp
                else:
                    from_p = jnp.logical_not(here | (col == ym))
                for kv in range(2):
                    block = jnp.where(from_p, yr[b, 1, n, kv], yr[b, 0, n, kv])
                    block = jnp.where(here, kvg[s][src, kv, slot], block)
                    parts[kv].append(block)
            for kv in range(2):
                for _ in range(l + 1, LEVELS):
                    parts[kv].append(jnp.zeros((BLK, DH), BF16))
            k_all = jnp.concatenate(parts[0], axis=0)
            v_all = jnp.concatenate(parts[1], axis=0)
            scores = lax.dot_general(
                q_rows, k_all, (((1,), (1,)), ((), ())), preferred_element_type=F32
            ) * DH ** (-0.5)
            scores = jnp.where(allowed, scores, masked_score)
            highest = jnp.max(scores, axis=1, keepdims=True)
            expo = jnp.exp(scores - highest)
            weights = (expo / jnp.sum(expo, axis=1, keepdims=True)).astype(BF16)
            got = jnp.dot(weights, v_all, preferred_element_type=F32).astype(BF16)
            rows = pl.ds(pl.multiple_of(n * BLK, BLK), BLK)
            for h in range(HEADS_HERE):
                ag[3, l, rows, h * DH : (h + 1) * DH] = got[h * BLK : (h + 1) * BLK]

        for half in range(2):

            def pair(i, carry):
                for j in range(2):
                    one(half * HALF + 2 * i + j, half)
                return carry

            lax.fori_loop(0, HALF // 2, pair, 0)
        own = ag.at[3, l]
        send(own, ag.at[0, l], xs.at[l, 0], xr.at[l, 0], at_xp)
        send(own, ag.at[1, l], xs.at[l, 1], xr.at[l, 1], at_xm)

    def x_pass(l):
        top, low = pl.ds(0, ROWS // 2), pl.ds(ROWS // 2, ROWS // 2)
        arrived(ag.at[0, l], xs.at[l, 0], xr.at[l, 0])
        send(ag.at[0, l, top], ag.at[2, l, top], xs.at[l, 2], xr.at[l, 2], at_xp)
        arrived(ag.at[1, l], xs.at[l, 1], xr.at[l, 1])
        send(ag.at[1, l, low], ag.at[2, l, low], xs.at[l, 3], xr.at[l, 3], at_xm)

    def x_end(l):
        arrived(ag.at[2, l, pl.ds(0, ROWS // 2)], xs.at[l, 2], xr.at[l, 2])
        arrived(ag.at[2, l, pl.ds(ROWS // 2, ROWS // 2)], xs.at[l, 3], xr.at[l, 3])

    def w_rows(yy, cc):
        return pl.ds(pl.multiple_of((yy * NC + cc) * WROWS, WROWS), WROWS)

    def w_start():
        rows = w_rows(y, c)
        for slot, to, dev in ((0, xp, at_xp), (1, xm, at_xm), (2, xa, at_xa)):
            cols = pl.ds(pl.multiple_of(to * WIDTH, WIDTH), WIDTH)
            send(w_hbm.at[rows, cols], wf.at[slot, rows], wxs.at[slot], wxr.at[slot], dev)

    three = pl.ds(0, 3)

    def w_mid():
        rows = w_rows(y, c)
        for slot in range(3):
            arrived(wf.at[slot, rows], wxs.at[slot], wxr.at[slot])
        piece = wf.at[three, rows]
        send(piece, piece, wys.at[0], wyr.at[0], at_yp)
        send(piece, piece, wys.at[1], wyr.at[1], at_ym)
        send(piece, piece, wbs.at[0], wbr.at[0], at_sib)

    def w_halves(yy, cc):
        base = (yy * NC + cc) * WROWS
        return (
            pl.ds(pl.multiple_of(base, WROWS // 2), WROWS // 2),
            pl.ds(pl.multiple_of(base + WROWS // 2, WROWS // 2), WROWS // 2),
        )

    def w_pass():
        for j, (yy, dev) in enumerate(((ym, at_yp), (yp, at_ym))):
            piece = wf.at[three, w_rows(yy, c)]
            arrived(piece, wys.at[j], wyr.at[j])
            onward = wf.at[three, w_halves(yy, c)[j]]
            send(onward, onward, wys.at[2 + j], wyr.at[2 + j], dev)
            send(piece, piece, wbs.at[1 + j], wbr.at[1 + j], at_sib)

    def w_last():
        for j in range(2):
            arrived(wf.at[three, w_halves(ya2, c)[j]], wys.at[2 + j], wyr.at[2 + j])
        piece = wf.at[three, w_rows(ya2, c)]
        send(piece, piece, wbs.at[3], wbr.at[3], at_sib)

    def w_end():
        for j, yy in enumerate((y, ym, yp, ya2)):
            arrived(wf.at[three, w_rows(yy, 1 - c)], wbs.at[j], wbr.at[j])
        in_w.wait()

    out_copies = []

    def project(l):
        sqacc[...] = jnp.zeros_like(sqacc)
        mxacc[...] = jnp.zeros_like(mxacc)

        def tile(j, carry):
            cols = pl.ds(pl.multiple_of(j * TILE, TILE), TILE)
            total = jnp.dot(ag[3, l], wf[3, :, cols], preferred_element_type=F32)
            for slot in range(3):
                total = total + jnp.dot(ag[slot, l], wf[slot, :, cols], preferred_element_type=F32)
            res = r_v[pl.ds(W * l, W), :, cols].reshape(ROWS, TILE)
            hid = (res.astype(F32) + total).astype(BF16)
            hid_v[pl.ds(W * l, W), :, cols] = hid.reshape(W, BLK, TILE)
            hid_f = hid.astype(F32)
            mixer = gain_ref[:, cols].astype(F32) * vw_ref[:, cols].astype(F32)
            square = hid_f * hid_f
            mixed = hid_f * mixer
            sqacc[...] += square[:, :128] + square[:, 128:]
            mxacc[...] += mixed[:, :128] + mixed[:, 128:]
            return carry

        lax.fori_loop(0, WIDTH // TILE, tile, 0)
        copy = local(hid_v.at[pl.ds(W * l, W)], hid_hbm.at[pl.ds(W * l, W)])
        out_copies.append(copy)
        for base, acc in ((0, sqacc), (8, mxacc)):
            for half in range(2):
                turned = acc[half * 128 : (half + 1) * 128].T
                stats[base + 2 * l + half : base + 2 * l + half + 1, :] = jnp.sum(turned, axis=0, keepdims=True)

    def family():
        parents = ap[...].reshape(NY * ZC, 128)
        pvm[0:64] = parents
        pvm[64:128] = jnp.full((64, 128), -1, jnp.int32)
        turned = pvm[...].T
        pd = lax.broadcasted_iota(jnp.int32, (64, 128), 0)
        lane = lax.broadcasted_iota(jnp.int32, (128, 128), 1)
        for l in range(3):
            for j in range(W):
                child = W * (l + 1) + j
                row = lax.shift_right_arithmetic(turned[child : child + 1, :], 5)
                amat[l, :, j * 128 : (j + 1) * 128] = jnp.where(
                    jnp.broadcast_to(row, (64, 128)) == pd, 1.0, 0.0
                ).astype(BF16)
                col = pvm[:, child : child + 1] & 31
                bmat[l, j * 128 : (j + 1) * 128, :] = jnp.where(
                    jnp.broadcast_to(col, (128, 128)) == lane, 1.0, 0.0
                )
            count = jnp.dot(amat[l], bmat[l].astype(BF16), preferred_element_type=F32)
            invm[l] = jnp.where(count > 0, 0.5 / jnp.maximum(count, 1.0), 0.0)
            keepm[l] = jnp.where(count > 0, 0.5, 1.0)

    def tail():
        for i, dev in enumerate((at_xp, at_xm, at_xa)):
            send(stats, srecv.at[i], sts.at[i], strv.at[i], dev)
        for i in range(3):
            arrived(srecv.at[i], sts.at[i], strv.at[i])
        total = (stats[...] + srecv[0]) + (srecv[1] + srecv[2])
        score = total[8:16] / jnp.sqrt(total[0:8] / D + norm_eps)
        jj = lax.broadcasted_iota(jnp.int32, (128, 128), 0)
        nn = lax.broadcasted_iota(jnp.int32, (128, 128), 1)
        group = jnp.where((jj // BLK) == (nn & 3), 1.0, 0.0)
        sums = jnp.dot(score, group, preferred_element_type=F32, precision=lax.Precision.HIGHEST)
        rr = lax.broadcasted_iota(jnp.int32, (8, 128), 0)
        ln = lax.broadcasted_iota(jnp.int32, (8, 128), 1)
        per_node = jnp.sum(jnp.where((ln // 4) == rr, sums, 0.0), axis=0, keepdims=True)
        reward = jnp.tanh(per_node / math.sqrt(BLK))
        wide = jnp.broadcast_to(reward, (8, 128))
        rtile[...] = jnp.where((rr == (zc & 7)) & (ln < counts_ref[0]), wide, 0.0)
        gather_send(rtile, gr, 1)
        gather_pass(rtile, gr, ar, 1)
        gather_end(ar, 1)
        values = ar[...].reshape(NY * ZC, 128)
        for l in (2, 1, 0):
            padded = jnp.concatenate([values, jnp.zeros((64, 128), F32)], axis=0)
            spread = jnp.concatenate(
                [
                    bmat[l, j * 128 : (j + 1) * 128, :]
                    * jnp.broadcast_to(padded[:, W * (l + 1) + j : W * (l + 1) + j + 1], (128, 128))
                    for j in range(W)
                ],
                axis=0,
            )
            high = spread.astype(BF16)
            rest = spread - high.astype(F32)
            mid = rest.astype(BF16)
            low = (rest - mid.astype(F32)).astype(BF16)
            summed = jnp.dot(amat[l], high, preferred_element_type=F32)
            summed = summed + jnp.dot(amat[l], mid, preferred_element_type=F32)
            summed = summed + jnp.dot(amat[l], low, preferred_element_type=F32)
            values = keepm[l] * values + invm[l] * summed
        who = lax.broadcasted_iota(jnp.int32, (64, 128), 0)
        bk_ref[...] = jnp.sum(jnp.where(who == leaf, values, 0.0), axis=0, keepdims=True)

    gather_send(ptile_ref, gp, 0)
    z_start(0)
    w_start()
    z_start(1)
    in_q.wait()
    in_k.wait()
    in_v.wait()
    attention(0)
    z_step(0, 1)
    gather_pass(ptile_ref, gp, ap, 0)
    z_step(1, 1)
    w_mid()
    z_step(0, 2)
    z_start(2)
    z_step(1, 2)
    z_step(0, 3)
    gather_end(ap, 0)
    pvm[0:64] = ap[...].reshape(NY * ZC, 128)
    to_smem = local(pvm.at[pl.ds(0, 64)], psm)
    z_step(1, 3)
    x_pass(0)
    z_step(0, 4)
    z_step(2, 1)
    w_pass()
    to_smem.wait()
    z_end(0)
    y_far(0)
    y_far(1)
    z_step(1, 4)
    z_step(2, 2)
    y_near(0)
    y_far(3)
    z_end(1)
    y_far(2)
    y_near(1)
    y_far(4)
    z_step(2, 3)
    w_last()
    y_near(2)
    y_end(0)
    attention(1)
    z_step(2, 4)
    y_near(3)
    z_end(2)
    y_far(5)
    y_near(4)
    x_pass(1)
    y_end(1)
    y_end(2)
    attention(2)
    y_near(5)
    in_r.wait()
    w_end()
    x_end(0)
    project(0)
    x_pass(2)
    x_end(1)
    project(1)
    y_end(3)
    y_end(4)
    y_end(5)
    attention(3)
    family()
    x_end(2)
    project(2)
    x_pass(3)
    x_end(3)
    project(3)
    tail()
    for copy in out_copies:
        copy.wait()
    for copy in started:
        copy.wait_send()


def body(queries, keys, values, resid, out_weight, norm_gain, value_weight, parent, counts):
    leaf = lax.axis_index("leaf")
    row = lax.broadcasted_iota(jnp.int32, (8, 128), 0)
    wide = jnp.pad(parent, (0, 128 - SLOTS))[None, :]
    ptile = jnp.where(row == lax.rem(leaf, 8), wide, 0)
    dma = pltpu.SemaphoreType.DMA
    vm = pltpu.VMEM
    scratch = [
        vm((SLOTS, BLK, COLS), BF16),
        vm((SLOTS, BLK, DH), BF16),
        vm((SLOTS, BLK, DH), BF16),
        vm((SLOTS, BLK, WIDTH), BF16),
        vm((4, COLS, WIDTH), BF16),
        vm((ZC, 2, W, BLK, DH), BF16),
        vm((ZC, 2, W, BLK, DH), BF16),
        vm((ZC, 2, W, BLK, DH), BF16),
        vm((4, LEVELS, ROWS, COLS), BF16),
        vm((6, W, 2, BLK, DH), BF16),
        vm((6, W, 2, BLK, DH), BF16),
        vm((6, W, 2, BLK, DH), BF16),
        vm((6, 2, HALF, 2, BLK, DH), BF16),
        vm((6, 2, W, 2, BLK, DH), BF16),
        vm((SLOTS, BLK, WIDTH), BF16),
        vm((ZC, 8, 128), jnp.int32),
        vm((NY, 2, 8, 128), jnp.int32),
        vm((ZC, 8, 128), F32),
        vm((NY, 2, 8, 128), F32),
        pltpu.SMEM((NY * ZC, 128), jnp.int32),
        vm((128, 128), jnp.int32),
        vm((3, 64, W * 128), BF16),
        vm((3, W * 128, 128), F32),
        vm((3, 64, 128), F32),
        vm((3, 64, 128), F32),
        vm((16, 128), F32),
        vm((3, 16, 128), F32),
        vm((8, 128), F32),
        vm((ROWS, 128), F32),
        vm((ROWS, 128), F32),
        dma((24,)),
        dma((3, 2, 4)), dma((3, 2, 4)),
        dma((3, 8)), dma((3, 8)),
        dma((6, 2)), dma((6, 2)),
        dma((6, 2)), dma((6, 2)),
        dma((4, 4)), dma((4, 4)),
        dma((3,)), dma((3,)),
        dma((4,)), dma((4,)),
        dma((4,)), dma((4,)),
        dma((2, ZC)), dma((2, ZC)),
        dma((2, 3)), dma((2, 3)),
        dma((3,)), dma((3,)),
    ]
    hbm = pl.BlockSpec(memory_space=pl.ANY)
    whole = pl.BlockSpec(memory_space=pltpu.VMEM)
    hidden, backed = pl.pallas_call(
        kernel,
        out_shape=(
            jax.ShapeDtypeStruct((SLOTS, BLK, WIDTH), BF16),
            jax.ShapeDtypeStruct((1, 128), F32),
        ),
        in_specs=[hbm, hbm, hbm, hbm, hbm, whole, whole, whole, pl.BlockSpec(memory_space=pltpu.SMEM)],
        out_specs=(hbm, whole),
        scratch_shapes=scratch,
        compiler_params=pltpu.CompilerParams(
            collective_id=0, has_side_effects=True, vmem_limit_bytes=56 * 1024 * 1024
        ),
    )(
        queries, keys, values, resid, out_weight,
        norm_gain.reshape(1, WIDTH), value_weight.reshape(1, WIDTH), ptile, counts,
    )
    alive = jnp.arange(SLOTS, dtype=jnp.int32) < counts[0]
    layer_out = jnp.where(alive[:, None, None], hidden, jnp.zeros_like(hidden))
    return (layer_out, backed[0, :SLOTS])


def solution(mesh):
    in_specs = (
        P("leaf", None, "tensor"),
        P("leaf", None, "tensor"),
        P("leaf", None, "tensor"),
        P("leaf", None, "tensor"),
        P("tensor", None),
        P("tensor"),
        P("tensor"),
        P("leaf"),
        P("leaf"),
    )
    out_specs = (P("leaf", None, "tensor"), P("leaf"))
    return jax.shard_map(body, mesh=mesh, in_specs=in_specs, out_specs=out_specs, check_vma=False)
```

time: 720 us -> 117 us (0.16)
  blocking collectives: 404 us -> 0 us
  waiting for transfers between devices: 221 us -> 0 us
  Pallas kernels: 0 us -> 108 us
  starting transfers between devices: 30.8 us -> 0 us
  other arithmetic: 20.3 us -> 3.79 us
  between operations: 15.7 us -> 1.31 us
  matrix products: 12.2 us -> 0 us
  local copies, waits for them, and re-layouts: 15.6 us -> 3.73 us
    unnamed x4 -> x0, blocking collectives: 397 us -> none
    reduce_scatter x1 -> x0, waiting for transfers between devices: 131 us -> none  [body(): lax.psum_scatter(partial_value, 'tensor', scatter_dimension=1, tiled=True)]
    pallas_call x0 -> x1, Pallas kernels: none -> 108 us  [body(): pl.pallas_call(kernel, out_shape=(jax.ShapeDtypeStruct((SLOTS, BLK, WIDTH...]
    all_to_all x4 -> x0, waiting for transfers between devices: 89.8 us -> none  [the longest x3 82.6 us: relay_round(): lax.all_to_all(outgoing, 'leaf', split_axis=0, concat_axis=0, tiled=True)]
    all_to_all x4 -> x0, starting transfers between devices: 30.6 us -> none  [the longest x3 17.4 us: relay_round(): lax.all_to_all(outgoing, 'leaf', split_axis=0, concat_axis=0, tiled=True)]
    dot_general x6 -> x0, matrix products: 12.2 us -> none  [the longest x1 8.08 us: body(): jnp.dot(attended, out_weight, preferred_element_type=jnp.float32)]
    gather x9 -> x0, local copies, waits for them, and re-layouts: 10.7 us -> none  [pick_rows(): taken = jnp.take(source_rows, clipped, axis=0)]
  transfers between devices with their start and end apart: 5 -> 0, of which waited for: 5 -> 0; matrix products, arithmetic and copies ran while one was open for 1% -> 0% of each run, Pallas kernels for 0% -> 0%
where the time goes in v1:
time: 117 us
  Pallas kernels  108 us (92%)
  other arithmetic  3.79 us (3%)
  local copies, waits for them, and re-layouts  3.73 us (3%)
  between operations  1.31 us (1%)
    pallas_call x1, Pallas kernels, body(): pl.pallas_call(kernel, out_shape=(jax.ShapeDtypeStruct((SLOTS, BLK, WIDTH...  108 us
    select_n x1, other arithmetic, body(): layer_out = jnp.where(alive[:, None, None], hidden, jnp.zeros_like(hidden))  3.12 us

profile of v1, /device:TPU:1, one launch (start us, length us, event | category | flops | bytes accessed | tf_op | source)
XLA Modules:
  0.0 116.6 jit_solution(16870106976310223739)
XLA Ops:
  1.3 0.7 pad.4
  2.0 0.7 broadcast_select_fusion.1.ptile_ref
  2.6 1.3 %reshape.15.gain_ref = bf16[1,1024]{1,0:T(2,128)(2,1)} reshape(bf16[1024]{0:T(1024)(128)(2,1)} %param.14) | data formatting | bytes 4096 | tf_op jit(solution)/shard_map/reshape | solution.py:560
  3.9 1.3 %reshape.16.vw_ref = bf16[1,1024]{1,0:T(2,128)(2,1)} reshape(bf16[1024]{0:T(1024)(128)(2,1)} %param.15) | data formatting | bytes 4096 | tf_op jit(solution)/shard_map/reshape | solution.py:560
  5.2 107.7 %shard_map.104 = (bf16[32,32,1024]{2,1,0:T(8,128)(2,1)}, f32[1,128]{1,0:T(1,128)}) custom-call(bf16[32,32,512]{2,1,0:T(8,128)(2,1)} %q_hbm.1, bf16[32,32,128]{2,1,0:T(8,128)(2,1)} %k_hbm.1, bf16[32,32,128]{2,1,0:T(8,128)(2,1)} %v_hbm.1, bf16[32,32,1024]{2,1,0:T(8,128)(2,1)} %r_hbm.1, bf16[512,4096]{1,0:T(8,128)(2,1)} %w_hbm.1, ...), custom_call_target="tpu_custom_call" | custom-call | tf_op jit(solution)/shard_map/pallas_call | solution.py:546
  112.9 0.0 copy-start
  112.9 3.1 %broadcast_select_fusion = bf16[32,32,1024]{2,1,0:T(8,128)(2,1)} fusion(bf16[32,32,1024]{2,1,0:T(8,128)(2,1)} %get-tuple-element.4, pred[32]{0:T(512)(128)(4,1)S(1)} %iota_compare_fusion.1), kind=kLoop, calls=%fused_computation | loop fusion | flops 1048576 | bytes 4194336 | tf_op jit(solution)/shard_map/jit(_where)/select_n | solution.py:563
  116.1 0.0 copy-done
  116.1 0.5 slice_bitcast_fusion
  (2 shorter events, 0.0 us)
Async XLA Ops:
  112.9 3.1 %copy-start = (f32[1,128]{1,0:T(1,128)S(1)}, f32[1,128]{1,0:T(1,128)}, u32[]{:S(2)}) copy-start(f32[1,128]{1,0:T(1,128)} %get-tuple-element.5) | copy-start | bytes 1540

commit v2 on v1

--- a/solution.py
+++ b/solution.py
@@ -32,12 +32,12 @@
 
 
 def kernel(
-    q_hbm, k_hbm, v_hbm, r_hbm, w_hbm, gain_ref, vw_ref, ptile_ref, counts_ref,
-    hid_hbm, bk_ref,
-    q_v, k_v, v_v, r_v, wf, kvg0, kvg1, kvg2, ag, ysa, ysp, ysm, yh, yr, hid_v,
-    gp, ap, gr, ar, psm, pvm, amat, bmat, invm, keepm, stats, srecv, rtile, sqacc, mxacc,
+    q_hbm, k_hbm, v_hbm, r_hbm, w_hbm, gain_ref, vw_ref, parent_ref, counts_ref,
+    hid_v, bk_ref,
+    q_v, k_v, v_v, r_v, wf, kvg0, kvg1, kvg2, ag, ysa, ysp, ysm, yh, yr,
+    ptl, pyr, pbuf, gr, gyr, psm, pvm, amat, bmat, invm, keepm, stats, srecv, rtile, sqacc, mxacc, mix,
     lsem, zs, zr, sbs, sbr, yas, yar, yfs, yfr, xs, xr, wxs, wxr, wys, wyr, wbs, wbr,
-    g1s, g1r, g2s, g2r, sts, strv,
+    pys, pyrv, ps, pr, pbs, pbr, gys, gyrv, gs, grv, sts, strv,
 ):
     kvg = (kvg0, kvg1, kvg2)
     leaf = lax.axis_index("leaf")
@@ -81,7 +81,7 @@
         remote(ref, ref, ssem, rsem, at_sib).wait_recv()
 
     barrier = pltpu.get_barrier_semaphore()
-    partners = [plane_peer(i) for i in range(1, ZC)] + [at_yp, at_ym, at_ya, at_xp, at_xm, at_xa]
+    partners = [at_zp, at_zm, at_sib, at_yp, at_ym, at_ya, at_xp, at_xm, at_xa]
     for dev in partners:
         pl.semaphore_signal(barrier, inc=1, device_id=dev, device_id_type=MESH)
 
@@ -108,51 +108,73 @@
     in_r = local(r_hbm, r_v)
     pl.semaphore_wait(barrier, len(partners))
 
-    def gather_send(tile, buf, which):
-        for i in range(1, ZC):
-            send(tile, buf.at[zc], g1s.at[which, i], g1r.at[which, i], plane_peer(i))
-
-    def gather_pass(tile, buf, whole, which):
-        buf[zc] = tile[...]
-        for i in range(1, ZC):
-            arrived(buf.at[lax.rem(zc + ZC - i, ZC)], g1s.at[which, i], g1r.at[which, i])
-        for half in range(2):
-            total = buf[8 * half]
-            for i in range(1, 8):
-                total = total + buf[8 * half + i]
-            whole[y, half] = total
-        send(whole.at[y], whole.at[y], g2s.at[which, 0], g2r.at[which, 0], at_yp)
-        send(whole.at[y], whole.at[y], g2s.at[which, 1], g2r.at[which, 1], at_ym)
-        send(whole.at[y], whole.at[y], g2s.at[which, 2], g2r.at[which, 2], at_ya)
-
-    def gather_end(whole, which):
-        arrived(whole.at[ym], g2s.at[which, 0], g2r.at[which, 0])
-        arrived(whole.at[yp], g2s.at[which, 1], g2r.at[which, 1])
-        arrived(whole.at[ya2], g2s.at[which, 2], g2r.at[which, 2])
+    sub = lax.broadcasted_iota(jnp.int32, (8, 128), 0)
+    ln = lax.broadcasted_iota(jnp.int32, (8, 128), 1)
+    mine_sub = sub == c * NY + y
+    mine_row = z * 8 + c * NY + y
+    y_peers = (at_yp, at_ym, at_ya)
+
+    def p_send():
+        row = jnp.zeros((8, 128), jnp.int32)
+        for n in range(SLOTS):
+            row = jnp.where(ln == n, parent_ref[n], row)
+        ptl[...] = jnp.where(mine_sub, row, 0)
+        for i, dev in enumerate(y_peers):
+            send(ptl, pyr.at[i], pys.at[i], pyrv.at[i], dev)
+
+    def p_start():
+        for i in range(3):
+            arrived(pyr.at[i], pys.at[i], pyrv.at[i])
+        pbuf[c, z] = (ptl[...] + pyr[0]) + (pyr[1] + pyr[2])
+        own = pbuf.at[c, z]
+        send(own, own, ps.at[0, 0], pr.at[0, 0], at_zp)
+        send(own, own, ps.at[1, 0], pr.at[1, 0], at_zm)
+
+    def p_step(s):
+        for way, d in ((0, -s), (1, s)):
+            if s == 4 and way == 1:
+                continue
+            one = pbuf.at[c, shift(z, d, NZ)]
+            arrived(one, ps.at[way, s - 1], pr.at[way, s - 1])
+            if s < 3 or (s == 3 and way == 0):
+                send(one, one, ps.at[way, s], pr.at[way, s], at_zm if way else at_zp)
+        if s == 4:
+            send(pbuf.at[c], pbuf.at[c], pbs, pbr, at_sib)
+
+    def p_end():
+        arrived(pbuf.at[1 - c], pbs, pbr)
+        parents = (pbuf[0] + pbuf[1]).reshape(64, 128)
+        pvm[0:64] = parents
+        pvm[64:128] = parents
+        return local(pvm.at[pl.ds(0, 64)], psm)
 
     def zidx(d, cc):
         return shift(z, d, NZ) * NC + cc
 
     def z_start(l):
-        for copy in own_kv[l]:
-            copy.wait()
+        for kv in range(2):
+            own_kv[l][kv].wait()
+            own = kvg[l].at[zc, kv]
+            send(own, own, zs.at[l, 0, 0, kv], zr.at[l, 0, 0, kv], at_zp)
+            send(own, own, zs.at[l, 1, 0, kv], zr.at[l, 1, 0, kv], at_zm)
         own = kvg[l].at[zc]
-        send(own, own, zs.at[l, 0, 0], zr.at[l, 0, 0], at_zp)
-        send(own, own, zs.at[l, 1, 0], zr.at[l, 1, 0], at_zm)
         send(own, own, sbs.at[l, 0], sbr.at[l, 0], at_sib)
 
     def z_step(l, s):
+        for kv in range(2):
+            for way, d in ((0, -s), (1, s)):
+                if s == 4 and kv != way:
+                    continue
+                piece = kvg[l].at[zidx(d, c), kv]
+                arrived(piece, zs.at[l, way, s - 1, kv], zr.at[l, way, s - 1, kv])
+                if s < 3 or (s == 3 and kv == way):
+                    send(piece, piece, zs.at[l, way, s, kv], zr.at[l, way, s, kv], at_zm if way else at_zp)
         for way, d in ((0, -s), (1, s)):
+            if s == 4 and way == 1:
+                continue
             shard = kvg[l].at[zidx(d, c)]
-            part = shard if s < 4 else shard.at[way]
-            arrived(part, zs.at[l, way, s - 1], zr.at[l, way, s - 1])
-            if s < 4:
-                onward = shard if s < 3 else shard.at[way]
-                send(onward, onward, zs.at[l, way, s], zr.at[l, way, s], at_zm if way else at_zp)
-                send(shard, shard, sbs.at[l, 1 + way * 3 + s - 1], sbr.at[l, 1 + way * 3 + s - 1], at_sib)
-        if s == 4:
-            shard = kvg[l].at[zidx(4, c)]
-            send(shard, shard, sbs.at[l, 7], sbr.at[l, 7], at_sib)
+            j = 7 if s == 4 else 1 + way * 3 + s - 1
+            send(shard, shard, sbs.at[l, j], sbr.at[l, j], at_sib)
 
     def z_end(l):
         for j, d in enumerate((0, -1, -2, -3, 1, 2, 3, 4)):
@@ -160,7 +182,9 @@
 
     def climb(node, hops):
         for _ in range(hops):
-            node = jnp.maximum(psm[lax.shift_right_logical(node, 5), node & 31], 0)
+            dev = lax.shift_right_logical(node, 5)
+            row = (lax.shift_right_logical(dev, 1) & 7) * 8 + (dev & 1) * NY + lax.shift_right_logical(dev, 4)
+            node = jnp.maximum(psm[row, node & 31], 0)
         return node
 
     def locate(dev, l, n, s):
@@ -321,8 +345,6 @@
             arrived(wf.at[three, w_rows(yy, 1 - c)], wbs.at[j], wbr.at[j])
         in_w.wait()
 
-    out_copies = []
-
     def project(l):
         sqacc[...] = jnp.zeros_like(sqacc)
         mxacc[...] = jnp.zeros_like(mxacc)
@@ -334,9 +356,12 @@
                 total = total + jnp.dot(ag[slot, l], wf[slot, :, cols], preferred_element_type=F32)
             res = r_v[pl.ds(W * l, W), :, cols].reshape(ROWS, TILE)
             hid = (res.astype(F32) + total).astype(BF16)
-            hid_v[pl.ds(W * l, W), :, cols] = hid.reshape(W, BLK, TILE)
+            node = W * l + lax.broadcasted_iota(jnp.int32, (W, BLK, TILE), 0)
+            hid_v[pl.ds(W * l, W), :, cols] = jnp.where(
+                node < counts_ref[0], hid.reshape(W, BLK, TILE), jnp.zeros((W, BLK, TILE), BF16)
+            )
             hid_f = hid.astype(F32)
-            mixer = gain_ref[:, cols].astype(F32) * vw_ref[:, cols].astype(F32)
+            mixer = mix[:, cols]
             square = hid_f * hid_f
             mixed = hid_f * mixer
             sqacc[...] += square[:, :128] + square[:, 128:]
@@ -344,31 +369,31 @@
             return carry
 
         lax.fori_loop(0, WIDTH // TILE, tile, 0)
-        copy = local(hid_v.at[pl.ds(W * l, W)], hid_hbm.at[pl.ds(W * l, W)])
-        out_copies.append(copy)
         for base, acc in ((0, sqacc), (8, mxacc)):
             for half in range(2):
                 turned = acc[half * 128 : (half + 1) * 128].T
                 stats[base + 2 * l + half : base + 2 * l + half + 1, :] = jnp.sum(turned, axis=0, keepdims=True)
 
     def family():
-        parents = ap[...].reshape(NY * ZC, 128)
-        pvm[0:64] = parents
-        pvm[64:128] = jnp.full((64, 128), -1, jnp.int32)
+        mix[...] = (gain_ref[...].astype(F32) * vw_ref[...].astype(F32)).reshape(1, WIDTH)
         turned = pvm[...].T
-        pd = lax.broadcasted_iota(jnp.int32, (64, 128), 0)
-        lane = lax.broadcasted_iota(jnp.int32, (128, 128), 1)
+        rows = lax.broadcasted_iota(jnp.int32, (64, 128), 0)
+        lanes = lax.broadcasted_iota(jnp.int32, (64, 128), 1)
+        first = lax.broadcasted_iota(jnp.int32, (1, 128), 1) < 64
         for l in range(3):
             for j in range(W):
                 child = W * (l + 1) + j
-                row = lax.shift_right_arithmetic(turned[child : child + 1, :], 5)
-                amat[l, :, j * 128 : (j + 1) * 128] = jnp.where(
-                    jnp.broadcast_to(row, (64, 128)) == pd, 1.0, 0.0
+                slot = pvm[0:64, child : child + 1] & 31
+                bmat[l, j * 64 : (j + 1) * 64, :] = jnp.where(jnp.broadcast_to(slot, (64, 128)) == lanes, 1.0, 0.0)
+            for j in range(0, W, 2):
+                child = W * (l + 1) + j
+                node = jnp.where(first, turned[child : child + 1, :], turned[child + 1 : child + 2, :])
+                dev = lax.shift_right_arithmetic(node, 5)
+                row = (lax.shift_right_arithmetic(dev, 1) & 7) * 8 + (dev & 1) * NY + lax.shift_right_arithmetic(dev, 4)
+                row = jnp.where(node < 0, -1, row)
+                amat[l, :, j * 64 : (j + 2) * 64] = jnp.where(
+                    jnp.broadcast_to(row, (64, 128)) == rows, 1.0, 0.0
                 ).astype(BF16)
-                col = pvm[:, child : child + 1] & 31
-                bmat[l, j * 128 : (j + 1) * 128, :] = jnp.where(
-                    jnp.broadcast_to(col, (128, 128)) == lane, 1.0, 0.0
-                )
             count = jnp.dot(amat[l], bmat[l].astype(BF16), preferred_element_type=F32)
             invm[l] = jnp.where(count > 0, 0.5 / jnp.maximum(count, 1.0), 0.0)
             keepm[l] = jnp.where(count > 0, 0.5, 1.0)
@@ -384,92 +409,96 @@
         nn = lax.broadcasted_iota(jnp.int32, (128, 128), 1)
         group = jnp.where((jj // BLK) == (nn & 3), 1.0, 0.0)
         sums = jnp.dot(score, group, preferred_element_type=F32, precision=lax.Precision.HIGHEST)
-        rr = lax.broadcasted_iota(jnp.int32, (8, 128), 0)
-        ln = lax.broadcasted_iota(jnp.int32, (8, 128), 1)
-        per_node = jnp.sum(jnp.where((ln // 4) == rr, sums, 0.0), axis=0, keepdims=True)
+        per_node = jnp.sum(jnp.where((ln // 4) == sub, sums, 0.0), axis=0, keepdims=True)
         reward = jnp.tanh(per_node / math.sqrt(BLK))
         wide = jnp.broadcast_to(reward, (8, 128))
-        rtile[...] = jnp.where((rr == (zc & 7)) & (ln < counts_ref[0]), wide, 0.0)
-        gather_send(rtile, gr, 1)
-        gather_pass(rtile, gr, ar, 1)
-        gather_end(ar, 1)
-        values = ar[...].reshape(NY * ZC, 128)
+        rtile[...] = jnp.where(mine_sub & (ln < counts_ref[0]), wide, 0.0)
+        for i, dev in enumerate(y_peers):
+            send(rtile, gyr.at[i], gys.at[i], gyrv.at[i], dev)
+        for i in range(3):
+            arrived(gyr.at[i], gys.at[i], gyrv.at[i])
+        gr[c, z] = (rtile[...] + gyr[0]) + (gyr[1] + gyr[2])
+        for i in range(1, ZC):
+            send(gr.at[c, z], gr.at[c, z], gs.at[i], grv.at[i], plane_peer(i))
+        for i in range(1, ZC):
+            other = lax.rem(zc + ZC - i, ZC)
+            arrived(gr.at[lax.rem(other, NC), other // NC], gs.at[i], grv.at[i])
+        values = (gr[0] + gr[1]).reshape(64, 128)
         for l in (2, 1, 0):
-            padded = jnp.concatenate([values, jnp.zeros((64, 128), F32)], axis=0)
             spread = jnp.concatenate(
                 [
-                    bmat[l, j * 128 : (j + 1) * 128, :]
-                    * jnp.broadcast_to(padded[:, W * (l + 1) + j : W * (l + 1) + j + 1], (128, 128))
+                    bmat[l, j * 64 : (j + 1) * 64, :]
+                    * jnp.broadcast_to(values[:, W * (l + 1) + j : W * (l + 1) + j + 1], (64, 128))
                     for j in range(W)
                 ],
                 axis=0,
             )
             high = spread.astype(BF16)
-            rest = spread - high.astype(F32)
-            mid = rest.astype(BF16)
-            low = (rest - mid.astype(F32)).astype(BF16)
+            low = (spread - high.astype(F32)).astype(BF16)
             summed = jnp.dot(amat[l], high, preferred_element_type=F32)
-            summed = summed + jnp.dot(amat[l], mid, preferred_element_type=F32)
             summed = summed + jnp.dot(amat[l], low, preferred_element_type=F32)
             values = keepm[l] * values + invm[l] * summed
         who = lax.broadcasted_iota(jnp.int32, (64, 128), 0)
-        bk_ref[...] = jnp.sum(jnp.where(who == leaf, values, 0.0), axis=0, keepdims=True)
-
-    gather_send(ptile_ref, gp, 0)
+        bk_ref[...] = jnp.sum(jnp.where(who == mine_row, values, 0.0), axis=0, keepdims=True)
+
     z_start(0)
+    p_send()
     w_start()
-    z_start(1)
     in_q.wait()
     in_k.wait()
     in_v.wait()
     attention(0)
     z_step(0, 1)
-    gather_pass(ptile_ref, gp, ap, 0)
-    z_step(1, 1)
+    p_start()
     w_mid()
     z_step(0, 2)
-    z_start(2)
-    z_step(1, 2)
+    p_step(1)
+    z_start(1)
     z_step(0, 3)
-    gather_end(ap, 0)
-    pvm[0:64] = ap[...].reshape(NY * ZC, 128)
-    to_smem = local(pvm.at[pl.ds(0, 64)], psm)
-    z_step(1, 3)
+    p_step(2)
+    p_step(3)
+    z_step(0, 4)
+    p_step(4)
+    z_step(1, 1)
     x_pass(0)
-    z_step(0, 4)
-    z_step(2, 1)
     w_pass()
+    to_smem = p_end()
+    z_end(0)
     to_smem.wait()
-    z_end(0)
     y_far(0)
     y_far(1)
+    z_step(1, 2)
+    z_start(2)
+    y_far(3)
+    y_near(0)
+    z_step(1, 3)
+    y_near(1)
     z_step(1, 4)
+    z_step(2, 1)
+    y_near(3)
+    w_last()
+    y_end(0)
+    attention(1)
     z_step(2, 2)
-    y_near(0)
-    y_far(3)
     z_end(1)
     y_far(2)
-    y_near(1)
     y_far(4)
     z_step(2, 3)
-    w_last()
     y_near(2)
-    y_end(0)
-    attention(1)
+    y_near(4)
     z_step(2, 4)
-    y_near(3)
-    z_end(2)
-    y_far(5)
-    y_near(4)
     x_pass(1)
     y_end(1)
     y_end(2)
     attention(2)
-    y_near(5)
+    z_end(2)
+    y_far(5)
+    family()
     in_r.wait()
     w_end()
     x_end(0)
     project(0)
+    y_near(5)
     x_pass(2)
     x_end(1)
     project(1)
@@ -477,24 +506,17 @@
     y_end(4)
     y_end(5)
     attention(3)
-    family()
     x_end(2)
     project(2)
     x_pass(3)
     x_end(3)
     project(3)
     tail()
-    for copy in out_copies:
-        copy.wait()
     for copy in started:
         copy.wait_send()
 
 
 def body(queries, keys, values, resid, out_weight, norm_gain, value_weight, parent, counts):
-    leaf = lax.axis_index("leaf")
-    row = lax.broadcasted_iota(jnp.int32, (8, 128), 0)
-    wide = jnp.pad(parent, (0, 128 - SLOTS))[None, :]
-    ptile = jnp.where(row == lax.rem(leaf, 8), wide, 0)
     dma = pltpu.SemaphoreType.DMA
     vm = pltpu.VMEM
     scratch = [
@@ -512,15 +534,15 @@
         vm((6, W, 2, BLK, DH), BF16),
         vm((6, 2, HALF, 2, BLK, DH), BF16),
         vm((6, 2, W, 2, BLK, DH), BF16),
-        vm((SLOTS, BLK, WIDTH), BF16),
-        vm((ZC, 8, 128), jnp.int32),
-        vm((NY, 2, 8, 128), jnp.int32),
-        vm((ZC, 8, 128), F32),
-        vm((NY, 2, 8, 128), F32),
-        pltpu.SMEM((NY * ZC, 128), jnp.int32),
+        vm((8, 128), jnp.int32),
+        vm((3, 8, 128), jnp.int32),
+        vm((NC, NZ, 8, 128), jnp.int32),
+        vm((NC, NZ, 8, 128), F32),
+        vm((3, 8, 128), F32),
+        pltpu.SMEM((64, 128), jnp.int32),
         vm((128, 128), jnp.int32),
-        vm((3, 64, W * 128), BF16),
-        vm((3, W * 128, 128), F32),
+        vm((3, 64, W * 64), BF16),
+        vm((3, W * 64, 128), F32),
         vm((3, 64, 128), F32),
         vm((3, 64, 128), F32),
         vm((16, 128), F32),
@@ -528,8 +550,9 @@
         vm((8, 128), F32),
         vm((ROWS, 128), F32),
         vm((ROWS, 128), F32),
+        vm((1, WIDTH), F32),
         dma((24,)),
-        dma((3, 2, 4)), dma((3, 2, 4)),
+        dma((3, 2, 4, 2)), dma((3, 2, 4, 2)),
         dma((3, 8)), dma((3, 8)),
         dma((6, 2)), dma((6, 2)),
         dma((6, 2)), dma((6, 2)),
@@ -537,31 +560,33 @@
         dma((3,)), dma((3,)),
         dma((4,)), dma((4,)),
         dma((4,)), dma((4,)),
-        dma((2, ZC)), dma((2, ZC)),
-        dma((2, 3)), dma((2, 3)),
+        dma((3,)), dma((3,)),
+        dma((2, 4)), dma((2, 4)),
+        dma(()), dma(()),
+        dma((3,)), dma((3,)),
+        dma((ZC,)), dma((ZC,)),
         dma((3,)), dma((3,)),
     ]
     hbm = pl.BlockSpec(memory_space=pl.ANY)
     whole = pl.BlockSpec(memory_space=pltpu.VMEM)
+    smem = pl.BlockSpec(memory_space=pltpu.SMEM)
     hidden, backed = pl.pallas_call(
         kernel,
         out_shape=(
-            jax.ShapeDtypeStruct((SLOTS, BLK, WIDTH), BF16),
-            jax.ShapeDtypeStruct((1, 128), F32),
+            pltpu.VMEM((SLOTS, BLK, WIDTH), BF16),
+            pltpu.VMEM((1, 128), F32),
         ),
-        in_specs=[hbm, hbm, hbm, hbm, hbm, whole, whole, whole, pl.BlockSpec(memory_space=pltpu.SMEM)],
-        out_specs=(hbm, whole),
+        in_specs=[hbm, hbm, hbm, hbm, hbm, whole, whole, smem, smem],
+        out_specs=(whole, whole),
         scratch_shapes=scratch,
         compiler_params=pltpu.CompilerParams(
             collective_id=0, has_side_effects=True, vmem_limit_bytes=56 * 1024 * 1024
         ),
     )(
         queries, keys, values, resid, out_weight,
-        norm_gain.reshape(1, WIDTH), value_weight.reshape(1, WIDTH), ptile, counts,
+        norm_gain, value_weight, parent, counts,
     )
-    alive = jnp.arange(SLOTS, dtype=jnp.int32) < counts[0]
-    layer_out = jnp.where(alive[:, None, None], hidden, jnp.zeros_like(hidden))
-    return (layer_out, backed[0, :SLOTS])
+    return (hidden, backed[0, :SLOTS])
 
 
 def solution(mesh):

time: 117 us -> 106 us (0.906)
  Pallas kernels: 108 us -> 103 us
  other arithmetic: 3.79 us -> 0 us
  local copies, waits for them, and re-layouts: 3.73 us -> 1.83 us
    pallas_call x1, Pallas kernels: 108 us -> 103 us  [body(): pl.pallas_call(kernel, out_shape=(pltpu.VMEM((SLOTS, BLK, WIDTH), BF16),...]
    select_n x2 -> x0, other arithmetic: 3.78 us -> none  [the longest x1 3.12 us: body(): layer_out = jnp.where(alive[:, None, None], hidden, jnp.zeros_like(hidden))]
    reshape x2 -> x0, local copies, waits for them, and re-layouts: 2.55 us -> none  [the longest x1 1.28 us: body(): value_weight.reshape(1, WIDTH)]
    unnamed x2 -> x1, local copies, waits for them, and re-layouts: 0.01 us -> 1.32 us
where the time goes in v2:
time: 106 us
  Pallas kernels  103 us (97%)
  local copies, waits for them, and re-layouts  1.83 us (2%)
  between operations  1.29 us (1%)
    pallas_call x1, Pallas kernels, body(): pl.pallas_call(kernel, out_shape=(pltpu.VMEM((SLOTS, BLK, WIDTH), BF16),...  103 us

profile of v2, /device:TPU:1, one launch (start us, length us, event | category | flops | bytes accessed | tf_op | source)
XLA Modules:
  0.0 105.6 jit_solution(12698544967101277262)
XLA Ops:
  1.3 102.5 %shard_map.104 = (bf16[32,32,1024]{2,1,0:T(8,128)(2,1)S(1)}, f32[1,128]{1,0:T(1,128)S(1)}) custom-call(bf16[32,32,512]{2,1,0:T(8,128)(2,1)} %q_hbm.1, bf16[32,32,128]{2,1,0:T(8,128)(2,1)} %k_hbm.1, bf16[32,32,128]{2,1,0:T(8,128)(2,1)} %v_hbm.1, bf16[32,32,1024]{2,1,0:T(8,128)(2,1)} %r_hbm.1, bf16[512,4096]{1,0:T(8,128)(2,1)} %w_hbm.1, ...), custom_call_target="tpu_custom_call" | custom-call | tf_op jit(solution)/shard_map/pallas_call | solution.py:573
  103.8 1.3 %copy.12 = bf16[32,32,1024]{2,1,0:T(8,128)(2,1)} copy(bf16[32,32,1024]{2,1,0:T(8,128)(2,1)S(1)} %get-tuple-element.6) | data formatting | bytes 4194304
  105.1 0.5 slice_bitcast_fusion

commit v3 on v2

--- a/solution.py
+++ b/solution.py
@@ -22,6 +22,7 @@
 WROWS = COLS // (NY * NC)
 TILE = 256
 HALF = W // 2
+GROUP = 4
 BATCHES = ((0, 1), (0, 2), (1, 2), (0, 3), (1, 3), (2, 3))
 
 norm_eps = 1e-05
@@ -35,7 +36,7 @@
     q_hbm, k_hbm, v_hbm, r_hbm, w_hbm, gain_ref, vw_ref, parent_ref, counts_ref,
     hid_v, bk_ref,
     q_v, k_v, v_v, r_v, wf, kvg0, kvg1, kvg2, ag, ysa, ysp, ysm, yh, yr,
-    ptl, pyr, pbuf, gr, gyr, psm, pvm, amat, bmat, invm, keepm, stats, srecv, rtile, sqacc, mxacc, mix,
+    ptl, pyr, pbuf, gr, gyr, psm, pvm, amat, bmat, invm, keepm, stats, srecv, rtile, sqacc, mxacc, mix, partial,
     lsem, zs, zr, sbs, sbr, yas, yar, yfs, yfr, xs, xr, wxs, wxr, wys, wyr, wbs, wbr,
     pys, pyrv, ps, pr, pbs, pbr, gys, gyrv, gs, grv, sts, strv,
 ):
@@ -61,9 +62,6 @@
     at_yp, at_ym, at_ya = (leaf_of(yp, z, c), x), (leaf_of(ym, z, c), x), (leaf_of(ya2, z, c), x)
     at_xp, at_xm, at_xa = (leaf, xp), (leaf, xm), (leaf, xa)
 
-    def plane_peer(i):
-        return (y * ZC + lax.rem(zc + i, ZC), x)
-
     started = []
 
     def remote(src, dst, ssem, rsem, dev):
@@ -76,6 +74,15 @@
         copy = remote(src, dst, ssem, rsem, dev)
         copy.start()
         started.append(copy)
+
+    def drain():
+        for copy in started:
+            copy.wait_send()
+        started.clear()
+
+    def drain_some(keep):
+        while len(started) > keep:
+            started.pop(0).wait_send()
 
     def arrived(ref, ssem, rsem):
         remote(ref, ref, ssem, rsem, at_sib).wait_recv()
@@ -132,13 +139,14 @@
 
     def p_step(s):
         for way, d in ((0, -s), (1, s)):
-            if s == 4 and way == 1:
-                continue
             one = pbuf.at[c, shift(z, d, NZ)]
             arrived(one, ps.at[way, s - 1], pr.at[way, s - 1])
-            if s < 3 or (s == 3 and way == 0):
+            if s < 3:
                 send(one, one, ps.at[way, s], pr.at[way, s], at_zm if way else at_zp)
-        if s == 4:
+            if s == 2 and way == 0:
+                send(one, one, ps.at[0, 3], pr.at[0, 3], (leaf_of(y, shift(z, 2, NZ), c), x))
+        if s == 3:
+            arrived(pbuf.at[c, shift(z, 4, NZ)], ps.at[0, 3], pr.at[0, 3])
             send(pbuf.at[c], pbuf.at[c], pbs, pbr, at_sib)
 
     def p_end():
@@ -151,30 +159,27 @@
     def zidx(d, cc):
         return shift(z, d, NZ) * NC + cc
 
-    def z_start(l):
-        for kv in range(2):
-            own_kv[l][kv].wait()
-            own = kvg[l].at[zc, kv]
-            send(own, own, zs.at[l, 0, 0, kv], zr.at[l, 0, 0, kv], at_zp)
-            send(own, own, zs.at[l, 1, 0, kv], zr.at[l, 1, 0, kv], at_zm)
-        own = kvg[l].at[zc]
-        send(own, own, sbs.at[l, 0], sbr.at[l, 0], at_sib)
-
-    def z_step(l, s):
-        for kv in range(2):
-            for way, d in ((0, -s), (1, s)):
-                if s == 4 and kv != way:
-                    continue
-                piece = kvg[l].at[zidx(d, c), kv]
-                arrived(piece, zs.at[l, way, s - 1, kv], zr.at[l, way, s - 1, kv])
-                if s < 3 or (s == 3 and kv == way):
-                    send(piece, piece, zs.at[l, way, s, kv], zr.at[l, way, s, kv], at_zm if way else at_zp)
+    def z_start(l, kv):
+        own_kv[l][kv].wait()
+        own = kvg[l].at[zc, kv]
+        send(own, own, zs.at[l, 0, 0, kv], zr.at[l, 0, 0, kv], at_zp)
+        send(own, own, zs.at[l, 1, 0, kv], zr.at[l, 1, 0, kv], at_zm)
+        if kv == 1:
+            own = kvg[l].at[zc]
+            send(own, own, sbs.at[l, 0], sbr.at[l, 0], at_sib)
+
+    def z_step(l, kv, s):
         for way, d in ((0, -s), (1, s)):
-            if s == 4 and way == 1:
+            if s == 4 and kv != way:
                 continue
             shard = kvg[l].at[zidx(d, c)]
-            j = 7 if s == 4 else 1 + way * 3 + s - 1
-            send(shard, shard, sbs.at[l, j], sbr.at[l, j], at_sib)
+            piece = shard.at[kv]
+            arrived(piece, zs.at[l, way, s - 1, kv], zr.at[l, way, s - 1, kv])
+            if s < 3 or (s == 3 and kv == way):
+                send(piece, piece, zs.at[l, way, s, kv], zr.at[l, way, s, kv], at_zm if way else at_zp)
+            if kv == 1:
+                j = 7 if s == 4 else 1 + way * 3 + s - 1
+                send(shard, shard, sbs.at[l, j], sbr.at[l, j], at_sib)
 
     def z_end(l):
         for j, d in enumerate((0, -1, -2, -3, 1, 2, 3, 4)):
@@ -209,13 +214,12 @@
 
     def y_near(b):
         s, l = BATCHES[b]
-        arrived(yh.at[b, 0], yas.at[b, 0], yar.at[b, 0])
-        arrived(yh.at[b, 1], yas.at[b, 1], yar.at[b, 1])
         dev_p = yp * ZC + zc
         dev_m = ym * ZC + zc
-
-        def pick(n, carry):
-            for half in range(2):
+        for half in range(2):
+            arrived(yh.at[b, half], yas.at[b, half], yar.at[b, half])
+
+            def pick(n, carry):
                 row = half * HALF + n
                 for out, dev, way in ((ysp, dev_p, 0), (ysm, dev_m, 1)):
                     col, src, slot = locate(dev, l, row, s)
@@ -224,15 +228,17 @@
                         if half == way:
                             mine = jnp.where(col == y, mine, yh[b, way, n, kv])
                         out[b, row, kv] = mine
-            return carry
-
-        lax.fori_loop(0, HALF, pick, 0)
-        send(ysp.at[b], yr.at[b, 0], yfs.at[b, 0], yfr.at[b, 0], at_yp)
-        send(ysm.at[b], yr.at[b, 1], yfs.at[b, 1], yfr.at[b, 1], at_ym)
-
-    def y_end(b):
-        arrived(yr.at[b, 0], yfs.at[b, 0], yfr.at[b, 0])
-        arrived(yr.at[b, 1], yfs.at[b, 1], yfr.at[b, 1])
+                return carry
+
+            lax.fori_loop(0, HALF, pick, 0)
+            rows = pl.ds(half * HALF, HALF)
+            send(ysp.at[b, rows], yr.at[b, 0, rows], yfs.at[b, 0, half], yfr.at[b, 0, half], at_yp)
+            send(ysm.at[b, rows], yr.at[b, 1, rows], yfs.at[b, 1, half], yfr.at[b, 1, half], at_ym)
+
+    def y_end(b, half):
+        rows = pl.ds(half * HALF, HALF)
+        for way in range(2):
+            arrived(yr.at[b, way, rows], yfs.at[b, way, half], yfr.at[b, way, half])
 
     row_q = lax.broadcasted_iota(jnp.int32, (HEADS_HERE * BLK, LEVELS * BLK), 0) & (BLK - 1)
     key_j = lax.broadcasted_iota(jnp.int32, (HEADS_HERE * BLK, LEVELS * BLK), 1)
@@ -241,7 +247,7 @@
         allowed = ((key_j < BLK) & (key_j <= row_q)) | ((key_j >= BLK) & (key_j < BLK * (l + 1)))
         mine_dev = leaf
 
-        def one(n, half):
+        def load(n, half):
             node = W * l + n
             q_node = q_v[node]
             q_rows = jnp.concatenate([q_node[:, h * DH : (h + 1) * DH] for h in range(HEADS_HERE)], axis=0)
@@ -262,42 +268,54 @@
             for kv in range(2):
                 for _ in range(l + 1, LEVELS):
                     parts[kv].append(jnp.zeros((BLK, DH), BF16))
-            k_all = jnp.concatenate(parts[0], axis=0)
-            v_all = jnp.concatenate(parts[1], axis=0)
-            scores = lax.dot_general(
-                q_rows, k_all, (((1,), (1,)), ((), ())), preferred_element_type=F32
-            ) * DH ** (-0.5)
-            scores = jnp.where(allowed, scores, masked_score)
+            return q_rows, jnp.concatenate(parts[0], axis=0), jnp.concatenate(parts[1], axis=0)
+
+        def weigh(scores):
+            scores = jnp.where(allowed, scores * DH ** (-0.5), masked_score)
             highest = jnp.max(scores, axis=1, keepdims=True)
             expo = jnp.exp(scores - highest)
-            weights = (expo / jnp.sum(expo, axis=1, keepdims=True)).astype(BF16)
-            got = jnp.dot(weights, v_all, preferred_element_type=F32).astype(BF16)
-            rows = pl.ds(pl.multiple_of(n * BLK, BLK), BLK)
-            for h in range(HEADS_HERE):
-                ag[3, l, rows, h * DH : (h + 1) * DH] = got[h * BLK : (h + 1) * BLK]
+            return (expo / jnp.sum(expo, axis=1, keepdims=True)).astype(BF16)
 
         for half in range(2):
-
-            def pair(i, carry):
-                for j in range(2):
-                    one(half * HALF + 2 * i + j, half)
+            for s in range(l):
+                y_end(BATCHES.index((s, l)), half)
+
+            def group(i, carry):
+                first = half * HALF + i * GROUP
+                loaded = [load(first + j, half) for j in range(GROUP)]
+                scores = [
+                    lax.dot_general(q, k, (((1,), (1,)), ((), ())), preferred_element_type=F32) for q, k, _ in loaded
+                ]
+                weights = [weigh(one) for one in scores]
+                for j in range(GROUP):
+                    got = jnp.dot(weights[j], loaded[j][2], preferred_element_type=F32).astype(BF16)
+                    rows = pl.ds(pl.multiple_of((first + j) * BLK, BLK), BLK)
+                    for h in range(HEADS_HERE):
+                        ag[3, l, rows, h * DH : (h + 1) * DH] = got[h * BLK : (h + 1) * BLK]
                 return carry
 
-            lax.fori_loop(0, HALF // 2, pair, 0)
-        own = ag.at[3, l]
-        send(own, ag.at[0, l], xs.at[l, 0], xr.at[l, 0], at_xp)
-        send(own, ag.at[1, l], xs.at[l, 1], xr.at[l, 1], at_xm)
-
-    def x_pass(l):
-        top, low = pl.ds(0, ROWS // 2), pl.ds(ROWS // 2, ROWS // 2)
-        arrived(ag.at[0, l], xs.at[l, 0], xr.at[l, 0])
-        send(ag.at[0, l, top], ag.at[2, l, top], xs.at[l, 2], xr.at[l, 2], at_xp)
-        arrived(ag.at[1, l], xs.at[l, 1], xr.at[l, 1])
-        send(ag.at[1, l, low], ag.at[2, l, low], xs.at[l, 3], xr.at[l, 3], at_xm)
+            lax.fori_loop(0, HALF // GROUP, group, 0)
+            rows = pl.ds(half * HALF * BLK, HALF * BLK)
+            own = ag.at[3, l, rows]
+            send(own, ag.at[0, l, rows], xs.at[l, half, 0], xr.at[l, half, 0], at_xp)
+            send(own, ag.at[1, l, rows], xs.at[l, half, 1], xr.at[l, half, 1], at_xm)
+
+    def x_parts(half):
+        quarter = HALF * BLK // 2
+        return pl.ds(half * 2 * quarter, quarter), pl.ds(half * 2 * quarter + quarter, quarter)
+
+    def x_pass(l, half):
+        rows = pl.ds(half * HALF * BLK, HALF * BLK)
+        top, low = x_parts(half)
+        arrived(ag.at[0, l, rows], xs.at[l, half, 0], xr.at[l, half, 0])
+        send(ag.at[0, l, top], ag.at[2, l, top], xs.at[l, half, 2], xr.at[l, half, 2], at_xp)
+        arrived(ag.at[1, l, rows], xs.at[l, half, 1], xr.at[l, half, 1])
+        send(ag.at[1, l, low], ag.at[2, l, low], xs.at[l, half, 3], xr.at[l, half, 3], at_xm)
 
     def x_end(l):
-        arrived(ag.at[2, l, pl.ds(0, ROWS // 2)], xs.at[l, 2], xr.at[l, 2])
-        arrived(ag.at[2, l, pl.ds(ROWS // 2, ROWS // 2)], xs.at[l, 3], xr.at[l, 3])
+        for half in range(2):
+            for way, part in enumerate(x_parts(half)):
+                arrived(ag.at[2, l, part], xs.at[l, half, 2 + way], xr.at[l, half, 2 + way])
 
     def w_rows(yy, cc):
         return pl.ds(pl.multiple_of((yy * NC + cc) * WROWS, WROWS), WROWS)
@@ -345,25 +363,32 @@
             arrived(wf.at[three, w_rows(yy, 1 - c)], wbs.at[j], wbr.at[j])
         in_w.wait()
 
-    def project(l):
+    def project_near(l):
+        def tile(j, carry):
+            cols = pl.ds(pl.multiple_of(j * TILE, TILE), TILE)
+            total = r_v[pl.ds(W * l, W), :, cols].reshape(ROWS, TILE).astype(F32)
+            for slot in (3, 0, 1):
+                total = total + jnp.dot(ag[slot, l], wf[slot, :, cols], preferred_element_type=F32)
+            partial[:, cols] = total
+            return carry
+
+        lax.fori_loop(0, WIDTH // TILE, tile, 0)
+
+    def project_far(l):
         sqacc[...] = jnp.zeros_like(sqacc)
         mxacc[...] = jnp.zeros_like(mxacc)
 
         def tile(j, carry):
             cols = pl.ds(pl.multiple_of(j * TILE, TILE), TILE)
-            total = jnp.dot(ag[3, l], wf[3, :, cols], preferred_element_type=F32)
-            for slot in range(3):
-                total = total + jnp.dot(ag[slot, l], wf[slot, :, cols], preferred_element_type=F32)
-            res = r_v[pl.ds(W * l, W), :, cols].reshape(ROWS, TILE)
-            hid = (res.astype(F32) + total).astype(BF16)
+            total = partial[:, cols] + jnp.dot(ag[2, l], wf[2, :, cols], preferred_element_type=F32)
+            hid = total.astype(BF16)
             node = W * l + lax.broadcasted_iota(jnp.int32, (W, BLK, TILE), 0)
             hid_v[pl.ds(W * l, W), :, cols] = jnp.where(
                 node < counts_ref[0], hid.reshape(W, BLK, TILE), jnp.zeros((W, BLK, TILE), BF16)
             )
             hid_f = hid.astype(F32)
-            mixer = mix[:, cols]
             square = hid_f * hid_f
-            mixed = hid_f * mixer
+            mixed = hid_f * mix[:, cols]
             sqacc[...] += square[:, :128] + square[:, 128:]
             mxacc[...] += mixed[:, :128] + mixed[:, 128:]
             return carry
@@ -401,6 +426,7 @@
     def tail():
         for i, dev in enumerate((at_xp, at_xm, at_xa)):
             send(stats, srecv.at[i], sts.at[i], strv.at[i], dev)
+        drain()
         for i in range(3):
             arrived(srecv.at[i], sts.at[i], strv.at[i])
         total = (stats[...] + srecv[0]) + (srecv[1] + srecv[2])
@@ -413,17 +439,21 @@
         reward = jnp.tanh(per_node / math.sqrt(BLK))
         wide = jnp.broadcast_to(reward, (8, 128))
         rtile[...] = jnp.where(mine_sub & (ln < counts_ref[0]), wide, 0.0)
-        for i, dev in enumerate(y_peers):
-            send(rtile, gyr.at[i], gys.at[i], gyrv.at[i], dev)
-        for i in range(3):
+        for i in range(1, 8):
+            yy, cc = shift(y, i // 2, NY), c if i % 2 == 0 else 1 - c
+            send(rtile, gyr.at[i], gys.at[i], gyrv.at[i], (leaf_of(yy, z, cc), x))
+        for i in range(1, 8):
             arrived(gyr.at[i], gys.at[i], gyrv.at[i])
-        gr[c, z] = (rtile[...] + gyr[0]) + (gyr[1] + gyr[2])
-        for i in range(1, ZC):
-            send(gr.at[c, z], gr.at[c, z], gs.at[i], grv.at[i], plane_peer(i))
-        for i in range(1, ZC):
-            other = lax.rem(zc + ZC - i, ZC)
-            arrived(gr.at[lax.rem(other, NC), other // NC], gs.at[i], grv.at[i])
-        values = (gr[0] + gr[1]).reshape(64, 128)
+        merged = rtile[...]
+        for i in range(1, 8):
+            merged = merged + gyr[i]
+        gr[z] = merged
+        for i in range(1, NZ):
+            send(gr.at[z], gr.at[z], gs.at[i], grv.at[i], (leaf_of(y, shift(z, i, NZ), c), x))
+        drain_some(7)
+        for i in range(1, NZ):
+            arrived(gr.at[shift(z, -i, NZ)], gs.at[i], grv.at[i])
+        values = gr[...].reshape(64, 128)
         for l in (2, 1, 0):
             spread = jnp.concatenate(
                 [
@@ -441,79 +471,94 @@
         who = lax.broadcasted_iota(jnp.int32, (64, 128), 0)
         bk_ref[...] = jnp.sum(jnp.where(who == mine_row, values, 0.0), axis=0, keepdims=True)
 
-    z_start(0)
     p_send()
+    z_start(0, 0)
+    z_start(0, 1)
+    z_start(1, 0)
     w_start()
+    p_start()
+    z_step(0, 0, 1)
+    z_step(0, 1, 1)
+    p_step(1)
+    z_step(1, 0, 1)
+    z_start(1, 1)
     in_q.wait()
     in_k.wait()
     in_v.wait()
     attention(0)
-    z_step(0, 1)
-    p_start()
     w_mid()
-    z_step(0, 2)
-    p_step(1)
-    z_start(1)
-    z_step(0, 3)
     p_step(2)
+    z_step(0, 0, 2)
+    z_step(0, 1, 2)
+    z_step(1, 0, 2)
+    z_step(1, 1, 1)
     p_step(3)
-    z_step(0, 4)
-    p_step(4)
-    z_step(1, 1)
-    x_pass(0)
+    z_step(0, 0, 3)
+    z_step(0, 1, 3)
+    z_step(1, 0, 3)
+    z_step(1, 1, 2)
+    z_start(2, 0)
+    z_start(2, 1)
+    to_smem = p_end()
+    x_pass(0, 0)
+    x_pass(0, 1)
+    z_step(0, 0, 4)
+    z_step(0, 1, 4)
     w_pass()
-    to_smem = p_end()
     z_end(0)
     to_smem.wait()
     y_far(0)
     y_far(1)
-    z_step(1, 2)
-    z_start(2)
+    z_step(1, 0, 4)
+    z_step(1, 1, 3)
+    z_step(2, 0, 1)
+    z_step(2, 1, 1)
     y_far(3)
+    z_step(1, 1, 4)
     y_near(0)
-    z_step(1, 3)
+    z_end(1)
+    z_step(2, 0, 2)
+    z_step(2, 1, 2)
+    y_far(2)
     y_near(1)
-    z_step(1, 4)
-    z_step(2, 1)
+    y_far(4)
+    z_step(2, 0, 3)
+    z_step(2, 1, 3)
+    w_last()
+    y_near(2)
+    attention(1)
+    z_step(2, 0, 4)
+    z_step(2, 1, 4)
     y_near(3)
-    w_last()
-    y_end(0)
-    attention(1)
-    z_step(2, 2)
-    z_end(1)
-    y_far(2)
-    y_far(4)
-    z_step(2, 3)
-    y_near(2)
-    y_near(4)
-    z_step(2, 4)
-    x_pass(1)
-    y_end(1)
-    y_end(2)
-    attention(2)
     z_end(2)
     y_far(5)
+    y_near(4)
+    attention(2)
+    x_pass(1, 0)
+    x_pass(1, 1)
+    y_near(5)
+    x_pass(2, 0)
+    x_pass(2, 1)
+    attention(3)
     family()
     in_r.wait()
     w_end()
+    project_near(0)
     x_end(0)
-    project(0)
-    y_near(5)
-    x_pass(2)
+    project_far(0)
+    x_pass(3, 0)
+    project_near(1)
     x_end(1)
-    project(1)
-    y_end(3)
-    y_end(4)
-    y_end(5)
-    attention(3)
+    project_far(1)
+    project_near(2)
     x_end(2)
-    project(2)
-    x_pass(3)
+    project_far(2)
+    x_pass(3, 1)
+    project_near(3)
     x_end(3)
-    project(3)
+    project_far(3)
     tail()
-    for copy in started:
-        copy.wait_send()
+    drain()
 
 
 def body(queries, keys, values, resid, out_weight, norm_gain, value_weight, parent, counts):
@@ -537,8 +582,8 @@
         vm((8, 128), jnp.int32),
         vm((3, 8, 128), jnp.int32),
         vm((NC, NZ, 8, 128), jnp.int32),
-        vm((NC, NZ, 8, 128), F32),
-        vm((3, 8, 128), F32),
+        vm((NZ, 8, 128), F32),
+        vm((8, 8, 128), F32),
         pltpu.SMEM((64, 128), jnp.int32),
         vm((128, 128), jnp.int32),
         vm((3, 64, W * 64), BF16),
@@ -551,20 +596,21 @@
         vm((ROWS, 128), F32),
         vm((ROWS, 128), F32),
         vm((1, WIDTH), F32),
+        vm((ROWS, WIDTH), F32),
         dma((24,)),
         dma((3, 2, 4, 2)), dma((3, 2, 4, 2)),
         dma((3, 8)), dma((3, 8)),
         dma((6, 2)), dma((6, 2)),
-        dma((6, 2)), dma((6, 2)),
-        dma((4, 4)), dma((4, 4)),
+        dma((6, 2, 2)), dma((6, 2, 2)),
+        dma((4, 2, 4)), dma((4, 2, 4)),
         dma((3,)), dma((3,)),
         dma((4,)), dma((4,)),
         dma((4,)), dma((4,)),
         dma((3,)), dma((3,)),
         dma((2, 4)), dma((2, 4)),
         dma(()), dma(()),
-        dma((3,)), dma((3,)),
-        dma((ZC,)), dma((ZC,)),
+        dma((8,)), dma((8,)),
+        dma((8,)), dma((8,)),
         dma((3,)), dma((3,)),
     ]
     hbm = pl.BlockSpec(memory_space=pl.ANY)

time: 106 us -> 98.7 us (0.931)
  Pallas kernels: 103 us -> 95.5 us
    pallas_call x1, Pallas kernels: 103 us -> 95.5 us  [body(): pl.pallas_call(kernel, out_shape=(pltpu.VMEM((SLOTS, BLK, WIDTH), BF16),...]
where the time goes in v3:
time: 98.7 us; the launch traced here: 98.6 us
  Pallas kernels  95.5 us (97%)
  local copies, waits for them, and re-layouts  1.83 us (2%)
  between operations  1.29 us (1%)
    pallas_call x1, Pallas kernels, body(): pl.pallas_call(kernel, out_shape=(pltpu.VMEM((SLOTS, BLK, WIDTH), BF16),...  95.5 us

profile of v3, /device:TPU:1, one launch (start us, length us, event | category | flops | bytes accessed | tf_op | source)
XLA Modules:
  0.0 98.6 jit_solution(14817834973630228539)
XLA Ops:
  1.3 95.5 %shard_map.104 = (bf16[32,32,1024]{2,1,0:T(8,128)(2,1)S(1)}, f32[1,128]{1,0:T(1,128)S(1)}) custom-call(bf16[32,32,512]{2,1,0:T(8,128)(2,1)} %q_hbm.1, bf16[32,32,128]{2,1,0:T(8,128)(2,1)} %k_hbm.1, bf16[32,32,128]{2,1,0:T(8,128)(2,1)} %v_hbm.1, bf16[32,32,1024]{2,1,0:T(8,128)(2,1)} %r_hbm.1, bf16[512,4096]{1,0:T(8,128)(2,1)} %w_hbm.1, ...), custom_call_target="tpu_custom_call" | custom-call | tf_op jit(solution)/shard_map/pallas_call | solution.py:619
  96.7 1.3 %copy.12 = bf16[32,32,1024]{2,1,0:T(8,128)(2,1)} copy(bf16[32,32,1024]{2,1,0:T(8,128)(2,1)S(1)} %get-tuple-element.6) | data formatting | bytes 4194304
  98.1 0.5 slice_bitcast_fusion

commit v4 on v3

--- a/solution.py
+++ b/solution.py
@@ -515,16 +515,15 @@
     z_step(2, 1, 1)
     y_far(3)
     z_step(1, 1, 4)
+    z_step(2, 0, 2)
+    z_step(2, 1, 2)
     y_near(0)
     z_end(1)
-    z_step(2, 0, 2)
-    z_step(2, 1, 2)
     y_far(2)
     y_near(1)
     y_far(4)
     z_step(2, 0, 3)
     z_step(2, 1, 3)
-    w_last()
     y_near(2)
     attention(1)
     z_step(2, 0, 4)
@@ -542,6 +541,7 @@
     attention(3)
     family()
     in_r.wait()
+    w_last()
     w_end()
     project_near(0)
     x_end(0)

time: 98.7 us -> 98 us (level)
  no operation moved by 1% of the time
where the time goes in v4:
time: 98 us; the launch traced here: 97.9 us
  Pallas kernels  94.8 us (97%)
  local copies, waits for them, and re-layouts  1.83 us (2%)
  between operations  1.29 us (1%)
    pallas_call x1, Pallas kernels, body(): pl.pallas_call(kernel, out_shape=(pltpu.VMEM((SLOTS, BLK, WIDTH), BF16),...  94.8 us

profile of v4, /device:TPU:1, one launch (start us, length us, event | category | flops | bytes accessed | tf_op | source)
XLA Modules:
  0.0 97.9 jit_solution(1321409811362081637)
XLA Ops:
  1.3 94.8 %shard_map.104 = (bf16[32,32,1024]{2,1,0:T(8,128)(2,1)S(1)}, f32[1,128]{1,0:T(1,128)S(1)}) custom-call(bf16[32,32,512]{2,1,0:T(8,128)(2,1)} %q_hbm.1, bf16[32,32,128]{2,1,0:T(8,128)(2,1)} %k_hbm.1, bf16[32,32,128]{2,1,0:T(8,128)(2,1)} %v_hbm.1, bf16[32,32,1024]{2,1,0:T(8,128)(2,1)} %r_hbm.1, bf16[512,4096]{1,0:T(8,128)(2,1)} %w_hbm.1, ...), custom_call_target="tpu_custom_call" | custom-call | tf_op jit(solution)/shard_map/pallas_call | solution.py:619
  96.1 1.3 %copy.12 = bf16[32,32,1024]{2,1,0:T(8,128)(2,1)} copy(bf16[32,32,1024]{2,1,0:T(8,128)(2,1)S(1)} %get-tuple-element.6) | data formatting | bytes 4194304
  97.4 0.5 slice_bitcast_fusion
